TPU v7x, 32 devices: a whole 2x2x4 slice. The times are simulated.
32 devices in a mesh: lat: 4 (over y, core), lon: 8 (over z, x).
Axes of the slice: x: 2, y: 2, z: 4, core: 2. Of those that a mesh axis runs over, the one named last changes fastest.
Arguments:
- signal: bfloat16 [32, 384, 1024], P(None, 'lat', 'lon'), may hold values from -6 to 6
- cotangent: bfloat16 [32, 384, 1024], P(None, 'lat', 'lon'), may hold values from -6 to 6
- edge_weights: bfloat16 [3, 384, 1024], P(None, 'lat', 'lon'), may hold values from 0.25 to 1
- circle_shift: int32 [384], P('lat'), may hold values from 0 to 1
- mixing: bfloat16 [6, 32, 32], replicated, may hold values from -0.4375 to 0.4375
Outputs:
- output: bfloat16 [32, 384, 1024], P(None, 'lat', 'lon')
- signal_grad: bfloat16 [32, 384, 1024], P(None, 'lat', 'lon')
- mixing_grad: float32 [6, 32, 32], replicated
All inputs are finite; a program needn't handle non-finite values.
Results may differ from a plain program's by a relative error of at most 0.0064.
Values may be sent and summed in bfloat16 or wider, within the bound.
No kernel may reach another device: no remote copies, remote signals or barrier semaphores. Data moves between devices by JAX's collectives and lax.ppermute only.
A program may use at most 128 MiB of HBM per device.

v0:
```python
import functools
import math

import jax
import jax.numpy as jnp
from jax import lax
from jax.experimental import pallas as pl
from jax.experimental.pallas import tpu as pltpu
from jax.sharding import PartitionSpec as P

F32 = jnp.float32
BF16 = jnp.bfloat16
HALO = 5
LANES = 128
BLOCKS = 4
GROUP = LANES // BLOCKS
SIDE = GROUP // 2
PACKED = 80
BAND = 3 * HALO
PACK_VMEM = 63_400_000


def params(mib):
    return pltpu.CompilerParams(vmem_limit_bytes=mib * 1024 * 1024)


def lane_index(shape):
    return lax.broadcasted_iota(jnp.int32, shape, len(shape) - 1)


def turned(x, amount):
    amount = amount % LANES
    return pltpu.roll(x, amount, 1) if amount else x


def spread_size(channels, rows):
    return rows * (3 * channels + 1)


def spread(wide, channels, c, rows, x):
    wide[pl.ds(3 * c, rows, stride=3 * channels + 1), :] = x


def gather(wide, channels, r, first, count):
    return wide[pl.ds(r * (3 * channels + 1) + 3 * first, count, stride=3), :]


def widen_all(signal, cotangent, weights, wide, ready=None):
    channels, rows, _ = signal.shape
    count = 2 * channels + 8
    for which, source in enumerate((signal, cotangent)):
        for part in range(4):
            if ready is not None:
                ready(which, part)
            for c in range(part * channels // 4, (part + 1) * channels // 4):
                spread(wide, count, which * channels + c, rows, source[c].astype(F32))
    if ready is not None:
        ready(2, 0)
    for i in range(8):
        x = weights[i].astype(F32) if i < 3 else jnp.zeros((rows, LANES), F32)
        spread(wide, count, 2 * channels + i, rows, x)


def row_loader(channels, rows, shift, wide):
    count = 2 * channels + 8
    sub = lax.broadcasted_iota(jnp.int32, (8, LANES), 0)

    def load_row(r):
        body = gather(wide, count, r, 0, 2 * channels)
        tail = gather(wide, count, r, 2 * channels, 8)
        parity = jnp.where(shift[r] == 1, 1.0, 0.0).astype(F32)
        tail = jnp.where(sub == 3, parity, tail)
        return jnp.concatenate([body, tail, jnp.zeros((8, LANES), F32)], axis=0).astype(BF16)

    return load_row


def pack_kernel(signal_hbm, cotangent_hbm, weights_hbm, shift, west_out, east_out,
                signal, cotangent, weights, wide, arrived):
    channels, rows, _ = signal.shape
    block = rows // BLOCKS
    per_row = block // 6
    size = channels // 4
    copies = {(2, 0): pltpu.make_async_copy(weights_hbm, weights, arrived.at[8])}
    for which, (source, target) in enumerate(((signal_hbm, signal), (cotangent_hbm, cotangent))):
        for part in range(4):
            span = pl.ds(part * size, size)
            copies[which, part] = pltpu.make_async_copy(source.at[span], target.at[span], arrived.at[4 * which + part])
    for copy in copies.values():
        copy.start()
    widen_all(signal, cotangent, weights, wide, lambda *key: copies[key].wait())
    load_row = row_loader(channels, rows, shift, wide)
    lane = lane_index((PACKED, LANES))

    def each(t, _):
        west = jnp.zeros((PACKED, LANES), BF16)
        east = jnp.zeros((PACKED, LANES), BF16)
        for b in range(BLOCKS):
            for m in range(6):
                x = load_row(block * b + per_row * m + t)
                first = GROUP * b + 5 * m
                moved = turned(x, first + 5)
                east = jnp.where((lane >= first) & (lane < first + 5), moved, east)
                west = jnp.where((lane - (first + 5)) % LANES < 5, moved, west)
        west_out[t] = west
        east_out[t] = east
        return 0

    lax.fori_loop(0, per_row, each, 0)


def strip_selector():
    source = lax.broadcasted_iota(jnp.int32, (BLOCKS * LANES, LANES), 0)
    lane = lane_index((BLOCKS * LANES, LANES))
    lane_in = lane % GROUP
    wanted = jnp.where(lane_in < SIDE, lane_in - 5, lane_in - SIDE + 117)
    wanted = jnp.where((lane_in >= 5) & (lane_in < SIDE + 11), wanted + LANES * (lane // GROUP), -1)
    return jnp.where(source == wanted, 1.0, 0.0).astype(BF16)


def own_kernel(signal, cotangent, weights_hbm, shift_hbm, mixing_hbm, strips_out, rows_out, mixing_out,
               wide, weights, shift, arrived):
    channels, rows, _ = signal.shape
    block = rows // BLOCKS
    copies = [pltpu.make_async_copy(source, target, arrived.at[i]) for i, (source, target) in enumerate(
        ((weights_hbm, weights), (shift_hbm, shift), (mixing_hbm, mixing_out)))]
    for copy in copies:
        copy.start()
    widen_all(signal, cotangent, weights, wide, lambda which, _: copies[0].wait() if which == 2 else None)
    copies[1].wait()
    load_row = row_loader(channels, rows, shift, wide)
    selector = strip_selector()
    size = 6

    def each(i, _):
        strips = []
        for j in range(size):
            s = i * size + j
            tiles = [load_row(block * b + s) for b in range(BLOCKS)]
            for b in range(BLOCKS):
                rows_out[block * b + s] = tiles[b]
            strips.append(side_by_side(tiles))
        strips = jnp.dot(jnp.concatenate(strips, axis=0), selector, preferred_element_type=F32).astype(BF16)
        for j in range(size):
            strips_out[i * size + j] = strips[PACKED * j:PACKED * (j + 1)]
        return 0

    lax.fori_loop(0, block // size, each, 0)
    copies[2].wait()


def merge_kernel(strips_in, rows_in, from_west, from_east, strips_out, north_out, south_out):
    block = strips_in.shape[0]
    rows = rows_in.shape[0]
    per_row = block // 6
    lane = lane_index((PACKED, LANES))
    lane_in = lane % GROUP

    def each(t, _):
        west = from_west[t]
        east = from_east[t]
        for m in range(6):
            strip = strips_in[per_row * m + t]
            strip = jnp.where(lane_in < 5, turned(west, -5 * m), strip)
            strip = jnp.where(lane_in >= GROUP - 5, turned(east, 22 - 5 * m), strip)
            strips_out[per_row * m + t] = strip
        return 0

    lax.fori_loop(0, per_row, each, 0)
    for out, first_row, first_strip, side in (
        (north_out, 0, 0, 0), (south_out, rows - HALO, block - HALO, BLOCKS - 1)):
        for i in range(HALO):
            out[i] = rows_in[first_row + i]
        corner = turned(strips_out[first_strip], -GROUP * side)
        for g in range(1, BLOCKS):
            piece = turned(strips_out[first_strip + g], GROUP * (g - side))
            corner = jnp.where((lane >= GROUP * g) & (lane < GROUP * (g + 1)), piece, corner)
        out[HALO] = corner
        out[HALO + 1] = turned(strips_out[first_strip + HALO - 1], -GROUP * side)


def write_coefficients(total, first, w_east, w_south, w_diag, parity, keep, coef, shifted):
    count = w_east.shape[0]
    w_back = jnp.where(parity > 0.5, turned(w_diag, 1), turned(w_diag, -1))
    w_west = turned(w_east, 1)
    shifted[0:8, :] = jnp.zeros((8, LANES), F32)
    shifted[8:8 + count, :] = w_south + w_back
    degree = w_east + w_west + w_south + w_diag + shifted[7:7 + count, :]
    third = -1.0 / 3.0
    arrays = [degree * (1.0 / 3.0) - 2.0, w_east * third, w_west * third]
    for array in (w_south, w_diag, w_back):
        arrays.append(array * third if keep is None else array * keep * third)
    for i, array in enumerate(arrays + [parity]):
        coef[i * total + first:i * total + first + count, :] = array


def stencil_steps(order, channels, total, coef, buffers, kept, trips, regions):
    groups = channels // 8

    def coef_row(i, at):
        return coef[pl.ds(i * total + at, 8, stride=0), :]

    def step(position, now, older, newer):
        last = position == order - 1

        def one_row(at, level, down, before):
            coefs = [coef_row(i, at) for i in range(7)]
            c, e, w, s, d, back, parity = coefs
            here = parity > 0.5
            s_above, d_above, above = before
            new, next_level, next_down = [], [], []
            for g in range(groups):
                span = slice(8 * g, 8 * g + 8)
                v = now[at, span, :]
                v_east = pltpu.roll(v, LANES - 1, 1)
                v_west = pltpu.roll(v, 1, 1)
                value = level[g] + s_above * v + d_above * jnp.where(above, v_east, v_west)
                new.append(value * 0.5 if position == 1 else value)
                value = c * v + e * v_east + w * v_west + down[g]
                next_level.append(value if position == 1 else value - older[at, span, :])
                next_down.append(s * v + back * jnp.where(here, v_west, v_east))
            if not last:
                for g in range(groups):
                    newer[at - 1, 8 * g:8 * g + 8, :] = new[g]
            for h in range(groups // 2):
                first = channels * position + 16 * h
                pair = jnp.concatenate([new[2 * h], new[2 * h + 1]], axis=0)
                kept[at - 1, first:first + 16, :] = pair.astype(BF16)
            return tuple(next_level), tuple(next_down), (s, d, here)

        counts = [-(-(count + 2 - 2 * position) // trips) for _, count in regions]

        def several(trip, carry):
            states = []
            for (base, _), count, (level, down) in zip(regions, counts, carry):
                at = base + position + trip * count
                before = (coef_row(3, at - 1), coef_row(4, at - 1), coef_row(6, at - 1) > 0.5)
                states.append([at, level, down, before])
            for j in range(max(counts)):
                for state, count in zip(states, counts):
                    if j < count:
                        state[1:] = one_row(state[0] + j, *state[1:])
            return tuple((level, down) for _, level, down, _ in states)

        zeros = tuple(jnp.zeros((8, LANES), F32) for _ in range(groups))
        lax.fori_loop(0, trips, several, tuple((zeros, zeros) for _ in regions))

    for position in range(1, order):
        step(position, buffers[(position - 1) % 3], buffers[(position - 2) % 3], buffers[position % 3])


def zero_guards(buffers, coef, total, guards):
    for first, end in guards:
        for index in range(first, end):
            for buffer in buffers:
                buffer[index] = jnp.zeros(buffer.shape[1:], F32)
        for i in range(7):
            coef[i * total + first:i * total + end, :] = jnp.zeros((end - first, LANES), F32)


CONTRACT_LANES = (((1,), (1,)), ((), ()))
CONTRACT_ROWS = (((0,), (0,)), ((), ()))


def side_by_side(tiles):
    return jnp.concatenate(tiles, axis=1)


class Chain:
    def __init__(self, first, other, mixing, guards, scratch):
        self.buffers, self.kept, self.coef, self.wide = scratch[:3], *scratch[3:6]
        self.paired = scratch[6] if other is not None else None
        self.first, self.other, self.mixing = first, other, mixing
        self.order, self.channels = mixing.shape[:2]
        self.total = self.kept.shape[0]
        for begin, end in guards:
            for index in range(begin, end):
                self.kept[index] = jnp.zeros((self.order * self.channels, LANES), BF16)
        zero_guards(self.buffers, self.coef, self.total, guards)
        for begin, end in guards:
            for i in range(4):
                at = i * (self.total + 1)
                self.wide[at + begin:at + end, :] = jnp.zeros((end - begin, LANES), F32)

    def put(self, index, ref, at, tile=None):
        def part(begin, count):
            return ref[at, begin:begin + count, :] if tile is None else tile[begin:begin + count]
        self.wide[pl.ds(index, 8, stride=self.total + 1), :] = part(PACKED - 16, 16).astype(F32)[:8]
        field = part(self.first, self.channels)
        self.buffers[0][index] = field.astype(F32)
        self.kept[index, 0:self.channels, :] = field
        if self.other is not None:
            self.paired[index] = part(self.other, self.channels)

    def put_all(self, index, ref, unroll):
        count = ref.shape[0]

        def several(i, _):
            for j in range(unroll):
                self.put(index + i * unroll + j, ref, i * unroll + j)
            return 0

        lax.fori_loop(0, count // unroll, several, 0)

    def put_strips(self, strips, north, south):
        block = strips.shape[0]
        self.put_all(1 + HALO, strips, block)
        lane = lane_index((PACKED, LANES))
        for i in range(HALO):
            at_end = i == HALO - 1
            above = turned(strips[block - HALO + i], GROUP)
            corner = turned(north[HALO + at_end], 0 if at_end else -GROUP * i)
            self.put(1 + i, None, None, jnp.where(lane < GROUP, corner, above))
            below = turned(strips[i], -GROUP)
            corner = turned(south[HALO + at_end], -GROUP - (0 if at_end else GROUP * i))
            self.put(1 + HALO + block + i, None, None, jnp.where(lane >= LANES - GROUP, corner, below))

    def run(self, trips, regions, closed=None):
        total = self.total
        starts = [i * (total + 1) for i in range(4)]
        w_east, w_south, w_diag, parity = [self.wide[at:at + total, :] for at in starts]
        keep = None
        if closed is not None:
            is_end, where = closed
            row = lax.broadcasted_iota(jnp.int32, (total, LANES), 0)
            keep = jnp.where(where(row, lane_index((total, LANES))) & is_end, 0.0, 1.0).astype(F32)
        write_coefficients(total, 0, w_east, w_south, w_diag, parity, keep, self.coef, self.wide)
        stencil_steps(self.order, self.channels, total, self.coef, self.buffers, self.kept, trips, regions)

    def terms(self, indices):
        return side_by_side([self.kept[i] for i in indices])

    def mixed(self, terms):
        if self.other is not None:
            matrix = self.mixing[...].reshape(self.order * self.channels, self.channels)
            value = lax.dot_general(matrix, terms, CONTRACT_ROWS, preferred_element_type=F32)
        else:
            matrix = side_by_side([self.mixing[k] for k in range(self.order)])
            value = jnp.dot(matrix, terms, preferred_element_type=F32)
        return value.astype(BF16)

    def paired_with(self, indices, valid, terms):
        left = [jnp.where(valid, self.paired[i], jnp.zeros((), BF16)) for i in indices]
        return lax.dot_general(side_by_side(left), terms, CONTRACT_LANES, preferred_element_type=F32)


def valid_lanes(channels):
    lane = lane_index((channels, LANES))
    lane_in = lane % GROUP
    in_strips = ((lane_in >= 5) & (lane_in < 10)) | ((lane_in >= SIDE + 6) & (lane_in < SIDE + 11))
    return (lane >= HALO) & (lane < LANES - HALO), in_strips


def main_forward(rows_in, mixing, out, grad, *scratch):
    rows = rows_in.shape[0]
    order, channels = mixing.shape[:2]
    chain = Chain(0, channels, mixing, ((0, 1), (rows + 1, rows + 8)), scratch)
    chain.put_all(1, rows_in, rows // 2)
    chain.run(2, ((0, rows),))
    valid, _ = valid_lanes(channels)

    def products(start, count, total_grad):
        indices = [start + 1 + i for i in range(count)]
        terms = chain.terms(indices)
        value = chain.mixed(terms)
        for i in range(count):
            out[start + i] = value[:, LANES * i:LANES * (i + 1)]
        return total_grad + chain.paired_with(indices, valid, terms)

    inner = rows - 2 * HALO
    total_grad = jnp.zeros(grad.shape, F32)
    half = inner // 2
    grad[...] = lax.fori_loop(0, 2, lambda i, g: products(HALO + i * half, half, g), total_grad)


def main_backward(is_last, rows_in, north, south, mixing, summed, out, summed_out, *scratch):
    rows = rows_in.shape[0]
    channels = mixing.shape[1]
    count = rows + 2 * HALO
    chain = Chain(channels, None, mixing, ((0, 1), (count + 1, scratch[0].shape[0])), scratch)
    for i in range(HALO):
        chain.put(1 + i, north, i)
        chain.put(1 + HALO + rows + i, south, i)
    chain.put_all(1 + HALO, rows_in, rows // 2)
    chain.run(2, ((0, count),), (is_last[0] == 1, lambda row, lane: row == HALO + rows))

    half = rows // 2

    def products(i, _):
        value = chain.mixed(chain.terms([1 + HALO + i * half + j for j in range(half)]))
        for j in range(half):
            out[i * half + j] = value[:, LANES * j:LANES * (j + 1)]
        return 0

    lax.fori_loop(0, 2, products, 0)
    summed_out[...] = summed[...]


def edge_sizes(rows):
    block = rows // BLOCKS
    strips = block + 2 * HALO
    top = strips + 6
    bottom = top + BAND + 5
    return block, top, bottom, -(-(bottom + BAND + 5) // 8) * 8


def edge_forward(is_last, strips_in, rows_in, north, south, mixing, out, grad, *scratch):
    rows = rows_in.shape[0]
    block, top, bottom, total = edge_sizes(rows)
    channels = mixing.shape[1]
    count = block + 2 * HALO
    chain = Chain(0, channels, mixing, ((0, 1), (1 + count, top + 1), (top + 1 + BAND, bottom + 1),
                                        (bottom + 1 + BAND, total)), scratch)
    chain.put_strips(strips_in, north, south)
    for i in range(HALO):
        chain.put(top + 1 + i, north, i)
        chain.put(bottom + 1 + 2 * HALO + i, south, i)
    for i in range(2 * HALO):
        chain.put(top + 1 + HALO + i, rows_in, i)
        chain.put(bottom + 1 + i, rows_in, rows - 2 * HALO + i)

    def closed(row, lane):
        return (row == bottom + 2 * HALO) | ((row == HALO + block) & (lane >= LANES - GROUP))

    chain.run(1, ((0, count), (top, BAND), (bottom, BAND)), (is_last[0] == 1, closed))
    main_valid, strip_valid = valid_lanes(channels)
    strip_rows = [1 + HALO + i for i in range(block)]
    band_rows = [top + 1 + HALO + i for i in range(HALO)] + [bottom + 1 + HALO + i for i in range(HALO)]
    total_grad = jnp.zeros(grad.shape, F32)
    slot = 0
    for indices, valid in ((strip_rows, strip_valid), (band_rows, main_valid)):
        terms = chain.terms(indices)
        value = chain.mixed(terms)
        for i in range(len(indices)):
            out[slot + i] = value[:, LANES * i:LANES * (i + 1)]
        slot += len(indices)
        total_grad = total_grad + chain.paired_with(indices, valid, terms)
    grad[...] = total_grad


def edge_backward(is_last, strips_in, north, south, mixing, summed, out, summed_out, *scratch):
    block = strips_in.shape[0]
    count = block + 2 * HALO
    chain = Chain(mixing.shape[1], None, mixing, ((0, 1), (1 + count, scratch[0].shape[0])), scratch)
    chain.put_strips(strips_in, north, south)
    chain.run(1, ((0, count),), (is_last[0] == 1, lambda row, lane: (row == HALO + block) & (lane >= LANES - GROUP)))
    value = chain.mixed(chain.terms([1 + HALO + i for i in range(block)]))
    for i in range(block):
        out[i] = value[:, LANES * i:LANES * (i + 1)]
    summed_out[...] = summed[...]


def assemble_kernel(main, edges, summed, out_hbm, summed_out, wide, out, sent):
    summed_out[...] = summed[...]
    rows, channels, _ = main.shape
    block = rows // BLOCKS
    lane = lane_index((channels, LANES))

    def put(r, s, b, value):
        strip = edges[s]
        west = turned(strip, -(GROUP * b + 5))
        east = turned(strip, LANES - 5 - (GROUP * b + SIDE + 6))
        value = jnp.where(lane < HALO, west, jnp.where(lane >= LANES - HALO, east, value))
        wide[pl.ds(r * (3 * channels + 1), channels, stride=3), :] = value.astype(F32)

    for b in range(BLOCKS):
        for s in range(block):
            put(block * b + s, s, b, main[block * b + s])
    if edges.shape[0] > block:
        for i in range(HALO):
            put(i, i, 0, edges[block + i])
            put(rows - HALO + i, block - HALO + i, BLOCKS - 1, edges[block + HALO + i])

    pieces = 2
    size = channels // pieces

    def narrow(i, _):
        for j in range(size):
            o = i * size + j
            out[o] = wide[pl.ds(3 * o, rows, stride=3 * channels + 1), :].astype(BF16)
        copy(i).start()
        return 0

    def copy(i):
        span = pl.ds(i * size, size)
        return pltpu.make_async_copy(out.at[span], out_hbm.at[span], sent.at[i])

    lax.fori_loop(0, pieces, narrow, 0)
    for i in range(pieces):
        copy(i).wait()


def finish_kernel(scale, mine, theirs, out):
    order, channels = out.shape[:2]
    out[...] = ((mine[...] + theirs[...]) * scale).T.reshape(order, channels, channels)


def on_device(signal, cotangent, edge_weights, circle_shift, mixing):
    channels, rows, sector = signal.shape
    order = mixing.shape[0]
    block, top, bottom, edge_total = edge_sizes(rows)
    lat, lon = lax.axis_size("lat"), lax.axis_size("lon")
    vmem = pl.BlockSpec(memory_space=pltpu.VMEM)
    smem = pl.BlockSpec(memory_space=pltpu.SMEM)
    hbm = pl.BlockSpec(memory_space=pltpu.HBM)
    shape = jax.ShapeDtypeStruct

    def packed(count):
        return shape((count, PACKED, LANES), BF16)

    def weighs(mib):
        return pl.CostEstimate(flops=0, bytes_accessed=mib * 1024 * 1024, transcendentals=0)

    all_wide = pltpu.VMEM((spread_size(2 * channels + 8, rows), LANES), F32)
    raw = (signal, cotangent, edge_weights, circle_shift)
    to_west, to_east = pl.pallas_call(
        pack_kernel,
        out_shape=(packed(block // 6), packed(block // 6)),
        in_specs=[hbm, hbm, hbm, smem],
        out_specs=(vmem, vmem),
        scratch_shapes=[
            pltpu.VMEM(signal.shape, BF16),
            pltpu.VMEM(signal.shape, BF16),
            pltpu.VMEM(edge_weights.shape, BF16),
            all_wide,
            pltpu.SemaphoreType.DMA((9,)),
        ],
        compiler_params=pltpu.CompilerParams(vmem_limit_bytes=PACK_VMEM),
        name="pack",
    )(*raw)

    eastward = [(i, (i + 1) % lon) for i in range(lon)]
    westward = [(j, i) for i, j in eastward]
    from_west = lax.ppermute(to_east, "lon", eastward)
    from_east = lax.ppermute(to_west, "lon", westward)

    own_strips, rows_in, mixing = pl.pallas_call(
        own_kernel,
        out_shape=(packed(block), packed(rows), shape(mixing.shape, BF16)),
        in_specs=[vmem, vmem, hbm, hbm, hbm],
        out_specs=(vmem, vmem, vmem),
        scratch_shapes=[
            all_wide,
            pltpu.VMEM(edge_weights.shape, BF16),
            pltpu.SMEM(circle_shift.shape, jnp.int32),
            pltpu.SemaphoreType.DMA((3,)),
        ],
        compiler_params=params(20),
        cost_estimate=weighs(8),
        name="own",
    )(*raw, mixing)

    strips, to_north, to_south = pl.pallas_call(
        merge_kernel,
        out_shape=(packed(block), packed(HALO + 2), packed(HALO + 2)),
        in_specs=[vmem] * 4,
        out_specs=(vmem,) * 3,
        compiler_params=params(8),
        name="merge",
    )(own_strips, rows_in, from_west, from_east)

    southward = [(i, i + 1) for i in range(lat - 1)]
    northward = [(j, i) for i, j in southward]
    north = lax.ppermute(to_south, "lat", southward)
    south = lax.ppermute(to_north, "lat", northward)

    rows_first = shape((rows, channels, LANES), BF16)
    grad_shape = shape((channels, order * channels), F32)

    def chain_scratch(total, with_pairs):
        scratch = [pltpu.VMEM((total, channels, LANES), F32)] * 3 + [
            pltpu.VMEM((total, order * channels, LANES), BF16),
            pltpu.VMEM((7 * total, LANES), F32),
            pltpu.VMEM((8 * (total + 1), LANES), F32),
        ]
        return scratch + [pltpu.VMEM((total, channels, LANES), BF16)] * with_pairs

    main_f, grad_main = pl.pallas_call(
        main_forward,
        out_shape=(rows_first, grad_shape),
        in_specs=[vmem, vmem],
        out_specs=(vmem, vmem),
        scratch_shapes=chain_scratch(rows + 8, True),
        compiler_params=params(20),
        cost_estimate=weighs(24),
        name="main_forward",
    )(rows_in, mixing)

    is_last = (lax.axis_index("lat") == lat - 1).astype(jnp.int32).reshape(1)
    edge_f, grad_edge = pl.pallas_call(
        edge_forward,
        out_shape=(shape((block + 2 * HALO, channels, LANES), BF16), grad_shape),
        in_specs=[smem] + [vmem] * 5,
        out_specs=(vmem, vmem),
        scratch_shapes=chain_scratch(edge_total, True),
        compiler_params=params(16),
        cost_estimate=weighs(12),
        name="edge_forward",
    )(is_last, strips, rows_in, north, south, mixing)

    rounds = []
    for axis, devices in (("lon", lon), ("lat", lat)):
        reach = 1
        while reach < devices:
            rounds.append((axis, [(i, i ^ reach) for i in range(devices)]))
            reach *= 2
    rounds = [r for r in rounds if r[0] == "lon"] + [r for r in rounds if r[0] == "lat"][::-1]

    results = {}

    def run_main_backward(share):
        results["main"], share = pl.pallas_call(
            main_backward,
            out_shape=(rows_first, grad_shape),
            in_specs=[smem] + [vmem] * 5,
            out_specs=(vmem, vmem),
            scratch_shapes=chain_scratch(-(-(rows + 2 * HALO + 8) // 8) * 8, False),
            compiler_params=params(20),
            cost_estimate=weighs(24),
            name="main_backward",
        )(is_last, rows_in, north, south, mixing, share)
        return share

    def run_edge_backward(share):
        results["edge"], share = pl.pallas_call(
            edge_backward,
            out_shape=(shape((block, channels, LANES), BF16), grad_shape),
            in_specs=[smem] + [vmem] * 5,
            out_specs=(vmem, vmem),
            scratch_shapes=chain_scratch(-(-(block + 2 * HALO + 8) // 8) * 8, False),
            compiler_params=params(12),
            cost_estimate=weighs(12),
            name="edge_backward",
        )(is_last, strips, north, south, mixing, share)
        return share

    def assemble(main, edges, share, name):
        return pl.pallas_call(
            assemble_kernel,
            out_shape=(shape(signal.shape, BF16), grad_shape),
            in_specs=[vmem] * 3,
            out_specs=(hbm, vmem),
            scratch_shapes=[
                pltpu.VMEM((spread_size(channels, rows), LANES), F32),
                pltpu.VMEM(signal.shape, BF16),
                pltpu.SemaphoreType.DMA((2,)),
            ],
            compiler_params=params(12),
            cost_estimate=weighs(8),
            name=name,
        )(main, edges, share)

    def run_assemble_forward(share):
        results["output"], share = assemble(main_f, edge_f, share, "assemble_forward")
        return share

    def run_assemble_backward(share):
        results["signal_grad"], share = assemble(results["main"], results["edge"], share, "assemble_backward")
        return share

    beside = [run_main_backward, run_assemble_forward, run_edge_backward, run_assemble_backward]
    share = grad_main + grad_edge
    theirs = jnp.zeros_like(share)
    for number in range(max(len(rounds), len(beside))):
        if number:
            share = share + theirs
        theirs = lax.ppermute(share, *rounds[number]) if number < len(rounds) else jnp.zeros_like(share)
        if number < len(beside):
            share = beside[number](share)

    norm_scale = 1.0 / math.sqrt(rows * lat * sector * lon)
    mixing_grad = pl.pallas_call(
        functools.partial(finish_kernel, norm_scale),
        out_shape=shape(mixing.shape, F32),
        in_specs=[vmem, vmem],
        out_specs=vmem,
        compiler_params=params(4),
        name="finish",
    )(share, theirs)
    return (results["output"], results["signal_grad"], mixing_grad)


def solution(mesh):
    in_specs = (P(None, "lat", "lon"), P(None, "lat", "lon"), P(None, "lat", "lon"), P("lat"), P())
    out_specs = (P(None, "lat", "lon"), P(None, "lat", "lon"), P())
    return jax.shard_map(
        on_device, mesh=mesh, in_specs=in_specs, out_specs=out_specs, check_vma=False
    )
```

profile of v0, /device:TPU:1, one launch (start us, length us, event | category | flops | bytes accessed | tf_op | source)
XLA Modules:
  0.0 54.8 jit_solution(4701954370371324158)
XLA Ops:
  0.6 3.9 %pack.1 = (bf16[4,80,128]{2,1,0:T(8,128)(2,1)}, bf16[4,80,128]{2,1,0:T(8,128)(2,1)}) custom-call(bf16[32,96,128]{2,1,0:T(8,128)(2,1)} %signal_hbm.1, bf16[32,96,128]{2,1,0:T(8,128)(2,1)} %cotangent_hbm.1, bf16[3,96,128]{2,1,0:T(8,128)(2,1)} %weights_hbm.3, s32[96]{0:T(128)} %shift.1), custom_call_target="tpu_custom_call" | custom-call | tf_op jit(solution)/shard_map/pack/pallas_call | solution.py:516
  4.5 2.1 %collective-permute-start = (bf16[4,80,128]{2,1,0:T(8,128)(2,1)}, bf16[4,80,128]{2,1,0:T(8,128)(2,1)S(1)}, u32[]{:S(2)}, u32[]{:S(2)}) collective-permute-start(bf16[4,80,128]{2,1,0:T(8,128)(2,1)} %get-tuple-element.27), channel_id=1, source_target_pairs={{0,1},{1,2},{2,3},{3,4},{4,5},{5,6},{6,7},{7,0},{8,9},{9,10},{10,1... | collective-permute-start | bytes 245768 | tf_op jit(solution)/shard_map/ppermute | solution.py:534
  6.6 3.1 %collective-permute-start.1 = (bf16[4,80,128]{2,1,0:T(8,128)(2,1)}, bf16[4,80,128]{2,1,0:T(8,128)(2,1)S(1)}, u32[]{:S(2)}, u32[]{:S(2)}) collective-permute-start(bf16[4,80,128]{2,1,0:T(8,128)(2,1)} %get-tuple-element.28), channel_id=1, source_target_pairs={{1,0},{2,1},{3,2},{4,3},{5,4},{6,5},{7,6},{0,7},{9,8},{10,9},{11,1... | collective-permute-start | bytes 245768 | tf_op jit(solution)/shard_map/ppermute | solution.py:535
  9.7 0.9 %copy-done.4 = bf16[3,96,128]{2,1,0:T(8,128)(2,1)S(1)} copy-done((bf16[3,96,128]{2,1,0:T(8,128)(2,1)S(1)}, bf16[3,96,128]{2,1,0:T(8,128)(2,1)}, u32[]{:S(2)}) %copy-start.4) | copy-done | bytes 73752
  10.6 0.8 %copy-done.5 = bf16[6,32,32]{2,1,0:T(8,128)(2,1)S(1)} copy-done((bf16[6,32,32]{2,1,0:T(8,128)(2,1)S(1)}, bf16[6,32,32]{2,1,0:T(8,128)(2,1)}, u32[]{:S(2)}) %copy-start.5) | copy-done | bytes 12312
  11.4 0.7 %copy-done.6 = s32[96]{0:T(128)S(1)} copy-done((s32[96]{0:T(128)S(1)}, s32[96]{0:T(128)}, u32[]{:S(2)}) %copy-start.6) | copy-done | bytes 408
  12.1 1.9 %own.1 = (bf16[24,80,128]{2,1,0:T(8,128)(2,1)S(1)}, bf16[96,80,128]{2,1,0:T(8,128)(2,1)S(1)}, bf16[6,32,32]{2,1,0:T(8,128)(2,1)S(1)}) custom-call(bf16[32,96,128]{2,1,0:T(8,128)(2,1)S(1)} %copy-done, bf16[32,96,128]{2,1,0:T(8,128)(2,1)S(1)} %copy-done.1, bf16[3,96,128]{2,1,0:T(8,128)(2,1)S(1)} %copy-done.4, s32[96]{0:T(128)S(1)} %copy-done.6, ...), custom_call_target="tpu_custom_call" | custom-call | bytes 8388608 | tf_op jit(solution)/shard_map/own/pallas_call | solution.py:537
  14.0 0.6 %merge.1 = (bf16[24,80,128]{2,1,0:T(8,128)(2,1)S(1)}, bf16[7,80,128]{2,1,0:T(8,128)(2,1)S(1)}, bf16[7,80,128]{2,1,0:T(8,128)(2,1)S(1)}) custom-call(bf16[24,80,128]{2,1,0:T(8,128)(2,1)S(1)} %get-tuple-element.26.strips_in, bf16[96,80,128]{2,1,0:T(8,128)(2,1)S(1)} %get-tuple-element.23.rows_in, bf16[4,80,128]{2,1,0:T(8,128)(2,1)S(1)} %collective-permute-done.from_west, ...), custom_call_target="tpu_custom_call" | custom-call | tf_op jit(solution)/shard_map/merge/pallas_call | solution.py:553
  14.7 4.1 %collective-permute-start.2 = (bf16[7,80,128]{2,1,0:T(8,128)(2,1)S(1)}, bf16[7,80,128]{2,1,0:T(8,128)(2,1)S(1)}, u32[]{:S(2)}, u32[]{:S(2)}) collective-permute-start(bf16[7,80,128]{2,1,0:T(8,128)(2,1)S(1)} %get-tuple-element.30), channel_id=1, source_target_pairs={{0,8},{8,16},{16,24},{1,9},{9,17},{17,25},{2,10},{10,18},{18,26},{... | collective-permute-start | bytes 430088 | tf_op jit(solution)/shard_map/ppermute | solution.py:564
  18.8 1.9 %collective-permute-start.3 = (bf16[7,80,128]{2,1,0:T(8,128)(2,1)S(1)}, bf16[7,80,128]{2,1,0:T(8,128)(2,1)S(1)}, u32[]{:S(2)}, u32[]{:S(2)}) collective-permute-start(bf16[7,80,128]{2,1,0:T(8,128)(2,1)S(1)} %get-tuple-element.31), channel_id=1, source_target_pairs={{8,0},{16,8},{24,16},{9,1},{17,9},{25,17},{10,2},{18,10},{26,18},{... | collective-permute-start | bytes 430088 | tf_op jit(solution)/shard_map/ppermute | solution.py:565
  20.7 0.8 %copy-done.3 = bf16[6,32,32]{2,1,0:T(8,128)(2,1)S(1)} copy-done((bf16[6,32,32]{2,1,0:T(8,128)(2,1)S(1)}, bf16[6,32,32]{2,1,0:T(8,128)(2,1)}, u32[]{:S(2)}) %copy-start.3) | copy-done | bytes 12312
  21.5 7.8 %main_forward.1 = (bf16[96,32,128]{2,1,0:T(8,128)(2,1)S(1)}, f32[32,192]{1,0:T(8,128)S(1)}) custom-call(bf16[96,80,128]{2,1,0:T(8,128)(2,1)S(1)} %get-tuple-element.23.rows_in, bf16[6,32,32]{2,1,0:T(8,128)(2,1)S(1)} %copy-done.3), custom_call_target="tpu_custom_call" | custom-call | bytes 25165824 | tf_op jit(solution)/shard_map/main_forward/pallas_call | solution.py:578
  29.4 3.6 %edge_forward.1 = (bf16[34,32,128]{2,1,0:T(8,128)(2,1)S(1)}, f32[32,192]{1,0:T(8,128)S(1)}) custom-call(s32[1]{0:T(128)} %bitcast.is_last, bf16[24,80,128]{2,1,0:T(8,128)(2,1)S(1)} %get-tuple-element.29.strips_in, bf16[96,80,128]{2,1,0:T(8,128)(2,1)S(1)} %get-tuple-element.23.rows_in, bf16[7,80,128]{2,1,0:T(8,128)(2,1)S(1)} %collective-permute-done.2.north, ...), custom_call_target="tpu_custom_call" | custom-call | bytes 12582912 | tf_op jit(solution)/shard_map/edge_forward/pallas_call | solution.py:590
  33.2 7.2 %main_backward.1 = (bf16[96,32,128]{2,1,0:T(8,128)(2,1)S(1)}, f32[32,192]{1,0:T(8,128)S(1)}) custom-call(s32[1]{0:T(128)} %bitcast.is_last, bf16[96,80,128]{2,1,0:T(8,128)(2,1)S(1)} %get-tuple-element.23.rows_in, bf16[7,80,128]{2,1,0:T(8,128)(2,1)S(1)} %collective-permute-done.2.north, bf16[7,80,128]{2,1,0:T(8,128)(2,1)S(1)} %collective-permute-done.3.south, ...), custom_call_target="tpu_custom_call" | custom-call | bytes 25165824 | tf_op jit(solution)/shard_map/main_backward/pallas_call | solution.py:612
  40.4 0.6 %collective-permute-start.5 = (f32[32,192]{1,0:T(8,128)S(1)}, f32[32,192]{1,0:T(8,128)S(1)}, u32[]{:S(2)}, u32[]{:S(2)}) collective-permute-start(f32[32,192]{1,0:T(8,128)S(1)} %add.16.summed), channel_id=1, source_target_pairs={{0,2},{1,3},{2,0},{3,1},{4,6},{5,7},{6,4},{7,5},{8,10},{9,11},{10,... | collective-permute-start | bytes 73736 | tf_op jit(solution)/shard_map/ppermute | solution.py:667
  41.0 1.5 %assemble_forward.1 = (bf16[32,96,128]{2,1,0:T(8,128)(2,1)}, f32[32,192]{1,0:T(8,128)S(1)}) custom-call(bf16[96,32,128]{2,1,0:T(8,128)(2,1)S(1)} %get-tuple-element.25.main, bf16[34,32,128]{2,1,0:T(8,128)(2,1)S(1)} %get-tuple-element.32.edges, f32[32,192]{1,0:T(8,128)S(1)} %add.16.summed), custom_call_target="tpu_custom_call" | custom-call | bytes 8388608 | tf_op jit(solution)/shard_map/assemble_forward/pallas_call | solution.py:638
  42.5 0.7 %collective-permute-done.5 = f32[32,192]{1,0:T(8,128)S(1)} collective-permute-done((f32[32,192]{1,0:T(8,128)S(1)}, f32[32,192]{1,0:T(8,128)S(1)}, u32[]{:S(2)}, u32[]{:S(2)}) %collective-permute-start.5) | collective-permute-done | bytes 24608 | tf_op jit(solution)/shard_map/ppermute | solution.py:667
  43.2 2.1 %collective-permute-start.6 = (f32[32,192]{1,0:T(8,128)S(1)}, f32[32,192]{1,0:T(8,128)S(1)}, u32[]{:S(2)}, u32[]{:S(2)}) collective-permute-start(f32[32,192]{1,0:T(8,128)S(1)} %add.17.summed), channel_id=1, source_target_pairs={{0,4},{1,5},{2,6},{3,7},{4,0},{5,1},{6,2},{7,3},{8,12},{9,13},{10,... | collective-permute-start | bytes 73736 | tf_op jit(solution)/shard_map/ppermute | solution.py:667
  45.3 1.9 %edge_backward.1 = (bf16[24,32,128]{2,1,0:T(8,128)(2,1)S(1)}, f32[32,192]{1,0:T(8,128)S(1)}) custom-call(s32[1]{0:T(128)} %bitcast.is_last, bf16[24,80,128]{2,1,0:T(8,128)(2,1)S(1)} %get-tuple-element.29.strips_in, bf16[7,80,128]{2,1,0:T(8,128)(2,1)S(1)} %collective-permute-done.2.north, bf16[7,80,128]{2,1,0:T(8,128)(2,1)S(1)} %collective-permute-done.3.south, ...), custom_call_target="tpu_custom_call" | custom-call | bytes 12582912 | tf_op jit(solution)/shard_map/edge_backward/pallas_call | solution.py:625
  47.4 1.4 %assemble_backward.1 = (bf16[32,96,128]{2,1,0:T(8,128)(2,1)}, f32[32,192]{1,0:T(8,128)S(1)}) custom-call(bf16[96,32,128]{2,1,0:T(8,128)(2,1)S(1)} %get-tuple-element.37.main, bf16[24,32,128]{2,1,0:T(8,128)(2,1)S(1)} %get-tuple-element.39.edges, f32[32,192]{1,0:T(8,128)S(1)} %add.18.summed), custom_call_target="tpu_custom_call" | custom-call | bytes 8388608 | tf_op jit(solution)/shard_map/assemble_backward/pallas_call | solution.py:638
  48.9 1.2 %collective-permute-done.7 = f32[32,192]{1,0:T(8,128)S(1)} collective-permute-done((f32[32,192]{1,0:T(8,128)S(1)}, f32[32,192]{1,0:T(8,128)S(1)}, u32[]{:S(2)}, u32[]{:S(2)}) %collective-permute-start.7) | collective-permute-done | bytes 24608 | tf_op jit(solution)/shard_map/ppermute | solution.py:667
  50.1 3.1 %collective-permute-start.8 = (f32[32,192]{1,0:T(8,128)S(1)}, f32[32,192]{1,0:T(8,128)S(1)}, u32[]{:S(2)}, u32[]{:S(2)}) collective-permute-start(f32[32,192]{1,0:T(8,128)S(1)} %add.19.mine), channel_id=1, source_target_pairs={{0,8},{8,0},{16,24},{24,16},{1,9},{9,1},{17,25},{25,17},{2,10},{10... | collective-permute-start | bytes 73736 | tf_op jit(solution)/shard_map/ppermute | solution.py:667
  53.2 0.9 %collective-permute-done.8.theirs = f32[32,192]{1,0:T(8,128)S(1)} collective-permute-done((f32[32,192]{1,0:T(8,128)S(1)}, f32[32,192]{1,0:T(8,128)S(1)}, u32[]{:S(2)}, u32[]{:S(2)}) %collective-permute-start.8) | collective-permute-done | bytes 24608 | tf_op jit(solution)/shard_map/ppermute | solution.py:667
  54.1 0.7 %finish.1 = f32[6,32,32]{2,1,0:T(8,128)} custom-call(f32[32,192]{1,0:T(8,128)S(1)} %add.19.mine, f32[32,192]{1,0:T(8,128)S(1)} %collective-permute-done.8.theirs), custom_call_target="tpu_custom_call" | custom-call | tf_op jit(solution)/shard_map/finish/pallas_call | solution.py:672
  (23 shorter events, 0.4 us)
Async XLA Ops:
  0.6 9.1 %copy-start.1 = (bf16[32,96,128]{2,1,0:T(8,128)(2,1)S(1)}, bf16[32,96,128]{2,1,0:T(8,128)(2,1)}, u32[]{:S(2)}) copy-start(bf16[32,96,128]{2,1,0:T(8,128)(2,1)} %cotangent_hbm.1) | copy-start | bytes 2359300
  0.6 9.1 %copy-start = (bf16[32,96,128]{2,1,0:T(8,128)(2,1)S(1)}, bf16[32,96,128]{2,1,0:T(8,128)(2,1)}, u32[]{:S(2)}) copy-start(bf16[32,96,128]{2,1,0:T(8,128)(2,1)} %signal_hbm.1) | copy-start | bytes 2359300
  4.5 9.5 %collective-permute-start = (bf16[4,80,128]{2,1,0:T(8,128)(2,1)}, bf16[4,80,128]{2,1,0:T(8,128)(2,1)S(1)}, u32[]{:S(2)}, u32[]{:S(2)}) collective-permute-start(bf16[4,80,128]{2,1,0:T(8,128)(2,1)} %get-tuple-element.27), channel_id=1, source_target_pairs={{0,1},{1,2},{2,3},{3,4},{4,5},{5,6},{6,7},{7,0},{8,9},{9,10},{10,1... | collective-permute-start | bytes 245768 | tf_op jit(solution)/shard_map/ppermute | solution.py:534
  6.6 7.4 %collective-permute-start.1 = (bf16[4,80,128]{2,1,0:T(8,128)(2,1)}, bf16[4,80,128]{2,1,0:T(8,128)(2,1)S(1)}, u32[]{:S(2)}, u32[]{:S(2)}) collective-permute-start(bf16[4,80,128]{2,1,0:T(8,128)(2,1)} %get-tuple-element.28), channel_id=1, source_target_pairs={{1,0},{2,1},{3,2},{4,3},{5,4},{6,5},{7,6},{0,7},{9,8},{10,9},{11,1... | collective-permute-start | bytes 245768 | tf_op jit(solution)/shard_map/ppermute | solution.py:535
  9.7 0.9 %copy-start.4 = (bf16[3,96,128]{2,1,0:T(8,128)(2,1)S(1)}, bf16[3,96,128]{2,1,0:T(8,128)(2,1)}, u32[]{:S(2)}) copy-start(bf16[3,96,128]{2,1,0:T(8,128)(2,1)} %weights_hbm.3) | copy-start | bytes 221188
  10.6 0.8 %copy-start.5 = (bf16[6,32,32]{2,1,0:T(8,128)(2,1)S(1)}, bf16[6,32,32]{2,1,0:T(8,128)(2,1)}, u32[]{:S(2)}) copy-start(bf16[6,32,32]{2,1,0:T(8,128)(2,1)} %mixing_hbm.1) | copy-start | bytes 36868
  11.4 0.7 %copy-start.6 = (s32[96]{0:T(128)S(1)}, s32[96]{0:T(128)}, u32[]{:S(2)}) copy-start(s32[96]{0:T(128)} %shift.1) | copy-start | bytes 1156
  14.0 4.8 %copy-start.2 = (bf16[6,32,32]{2,1,0:T(8,128)(2,1)}, bf16[6,32,32]{2,1,0:T(8,128)(2,1)S(1)}, u32[]{:S(2)}) copy-start(bf16[6,32,32]{2,1,0:T(8,128)(2,1)S(1)} %get-tuple-element.24.mixing) | copy-start | bytes 36868
  14.7 14.7 %collective-permute-start.2 = (bf16[7,80,128]{2,1,0:T(8,128)(2,1)S(1)}, bf16[7,80,128]{2,1,0:T(8,128)(2,1)S(1)}, u32[]{:S(2)}, u32[]{:S(2)}) collective-permute-start(bf16[7,80,128]{2,1,0:T(8,128)(2,1)S(1)} %get-tuple-element.30), channel_id=1, source_target_pairs={{0,8},{8,16},{16,24},{1,9},{9,17},{17,25},{2,10},{10,18},{18,26},{... | collective-permute-start | bytes 430088 | tf_op jit(solution)/shard_map/ppermute | solution.py:564
  18.8 10.6 %collective-permute-start.3 = (bf16[7,80,128]{2,1,0:T(8,128)(2,1)S(1)}, bf16[7,80,128]{2,1,0:T(8,128)(2,1)S(1)}, u32[]{:S(2)}, u32[]{:S(2)}) collective-permute-start(bf16[7,80,128]{2,1,0:T(8,128)(2,1)S(1)} %get-tuple-element.31), channel_id=1, source_target_pairs={{8,0},{16,8},{24,16},{9,1},{17,9},{25,17},{10,2},{18,10},{26,18},{... | collective-permute-start | bytes 430088 | tf_op jit(solution)/shard_map/ppermute | solution.py:565
  20.7 0.8 %copy-start.3 = (bf16[6,32,32]{2,1,0:T(8,128)(2,1)S(1)}, bf16[6,32,32]{2,1,0:T(8,128)(2,1)}, u32[]{:S(2)}) copy-start(bf16[6,32,32]{2,1,0:T(8,128)(2,1)} %copy-done.2) | copy-start | bytes 36868
  33.1 7.3 %collective-permute-start.4 = (f32[32,192]{1,0:T(8,128)S(1)}, f32[32,192]{1,0:T(8,128)S(1)}, u32[]{:S(2)}, u32[]{:S(2)}) collective-permute-start(f32[32,192]{1,0:T(8,128)S(1)} %add.15.summed), channel_id=1, source_target_pairs={{0,1},{1,0},{2,3},{3,2},{4,5},{5,4},{6,7},{7,6},{8,9},{9,8},{10,11... | collective-permute-start | bytes 73736 | tf_op jit(solution)/shard_map/ppermute | solution.py:667
  40.4 2.8 %collective-permute-start.5 = (f32[32,192]{1,0:T(8,128)S(1)}, f32[32,192]{1,0:T(8,128)S(1)}, u32[]{:S(2)}, u32[]{:S(2)}) collective-permute-start(f32[32,192]{1,0:T(8,128)S(1)} %add.16.summed), channel_id=1, source_target_pairs={{0,2},{1,3},{2,0},{3,1},{4,6},{5,7},{6,4},{7,5},{8,10},{9,11},{10,... | collective-permute-start | bytes 73736 | tf_op jit(solution)/shard_map/ppermute | solution.py:667
  43.2 4.0 %collective-permute-start.6 = (f32[32,192]{1,0:T(8,128)S(1)}, f32[32,192]{1,0:T(8,128)S(1)}, u32[]{:S(2)}, u32[]{:S(2)}) collective-permute-start(f32[32,192]{1,0:T(8,128)S(1)} %add.17.summed), channel_id=1, source_target_pairs={{0,4},{1,5},{2,6},{3,7},{4,0},{5,1},{6,2},{7,3},{8,12},{9,13},{10,... | collective-permute-start | bytes 73736 | tf_op jit(solution)/shard_map/ppermute | solution.py:667
  47.2 2.8 %collective-permute-start.7 = (f32[32,192]{1,0:T(8,128)S(1)}, f32[32,192]{1,0:T(8,128)S(1)}, u32[]{:S(2)}, u32[]{:S(2)}) collective-permute-start(f32[32,192]{1,0:T(8,128)S(1)} %add.18.summed), channel_id=1, source_target_pairs={{0,16},{8,24},{16,0},{24,8},{1,17},{9,25},{17,1},{25,9},{2,18},{10... | collective-permute-start | bytes 73736 | tf_op jit(solution)/shard_map/ppermute | solution.py:667
  50.1 4.0 %collective-permute-start.8 = (f32[32,192]{1,0:T(8,128)S(1)}, f32[32,192]{1,0:T(8,128)S(1)}, u32[]{:S(2)}, u32[]{:S(2)}) collective-permute-start(f32[32,192]{1,0:T(8,128)S(1)} %add.19.mine), channel_id=1, source_target_pairs={{0,8},{8,0},{16,24},{24,16},{1,9},{9,1},{17,25},{25,17},{2,10},{10... | collective-permute-start | bytes 73736 | tf_op jit(solution)/shard_map/ppermute | solution.py:667
where the time goes:
time: 55.5 us; the launch traced here: 54.8 us
  Pallas kernels  30.6 us (55%)
  starting transfers between devices  17.4 us (31%)
  local copies, waits for them, and re-layouts  3.15 us (6%)
  waiting for transfers between devices  2.87 us (5%)
  between operations  0.84 us (2%)
    pallas_call x1, Pallas kernels, on_device(): pl.pallas_call(main_forward, out_shape=(rows_first, grad_shape), in_specs...  7.82 us
    pallas_call x1, Pallas kernels, run_main_backward(): pl.pallas_call(main_backward, out_shape=(rows_first, grad_shape), in_spec...  7.19 us
    ppermute x5, starting transfers between devices, on_device(): lax.ppermute(share, *rounds[number])  6.12 us
    ppermute x1, starting transfers between devices, on_device(): north = lax.ppermute(to_south, 'lat', southward)  4.12 us
    pallas_call x1, Pallas kernels, on_device(): pl.pallas_call(pack_kernel, out_shape=(packed(block // 6), packed(block /...  3.88 us
    pallas_call x1, Pallas kernels, on_device(): pl.pallas_call(edge_forward, out_shape=(shape((block + 2 * HALO, channels...  3.64 us
    unnamed x14, local copies, waits for them, and re-layouts  3.15 us
    ppermute x1, starting transfers between devices, on_device(): from_east = lax.ppermute(to_west, 'lon', westward)  3.1 us
  transfers between devices with their start and end apart: 9, of which 3 were waited for; matrix products, arithmetic and copies ran while one was open for 0% of the time, Pallas kernels for 40%

commit v1 on v0

--- a/solution.py
+++ b/solution.py
@@ -75,40 +75,6 @@
     return load_row
 
 
-def pack_kernel(signal_hbm, cotangent_hbm, weights_hbm, shift, west_out, east_out,
-                signal, cotangent, weights, wide, arrived):
-    channels, rows, _ = signal.shape
-    block = rows // BLOCKS
-    per_row = block // 6
-    size = channels // 4
-    copies = {(2, 0): pltpu.make_async_copy(weights_hbm, weights, arrived.at[8])}
-    for which, (source, target) in enumerate(((signal_hbm, signal), (cotangent_hbm, cotangent))):
-        for part in range(4):
-            span = pl.ds(part * size, size)
-            copies[which, part] = pltpu.make_async_copy(source.at[span], target.at[span], arrived.at[4 * which + part])
-    for copy in copies.values():
-        copy.start()
-    widen_all(signal, cotangent, weights, wide, lambda *key: copies[key].wait())
-    load_row = row_loader(channels, rows, shift, wide)
-    lane = lane_index((PACKED, LANES))
-
-    def each(t, _):
-        west = jnp.zeros((PACKED, LANES), BF16)
-        east = jnp.zeros((PACKED, LANES), BF16)
-        for b in range(BLOCKS):
-            for m in range(6):
-                x = load_row(block * b + per_row * m + t)
-                first = GROUP * b + 5 * m
-                moved = turned(x, first + 5)
-                east = jnp.where((lane >= first) & (lane < first + 5), moved, east)
-                west = jnp.where((lane - (first + 5)) % LANES < 5, moved, west)
-        west_out[t] = west
-        east_out[t] = east
-        return 0
-
-    lax.fori_loop(0, per_row, each, 0)
-
-
 def strip_selector():
     source = lax.broadcasted_iota(jnp.int32, (BLOCKS * LANES, LANES), 0)
     lane = lane_index((BLOCKS * LANES, LANES))
@@ -118,40 +84,77 @@
     return jnp.where(source == wanted, 1.0, 0.0).astype(BF16)
 
 
-def own_kernel(signal, cotangent, weights_hbm, shift_hbm, mixing_hbm, strips_out, rows_out, mixing_out,
-               wide, weights, shift, arrived):
+EXTRA = 4
+
+
+def head_kernel(signal_hbm, cotangent_hbm, weights_hbm, shift_hbm, mixing_hbm, west_hbm, east_hbm, strips_hbm, rows_hbm,
+                signal, cotangent, weights, shift, mixing, wide, west_out, east_out, strips_out, rows_out, arrived, sent):
     channels, rows, _ = signal.shape
     block = rows // BLOCKS
-    copies = [pltpu.make_async_copy(source, target, arrived.at[i]) for i, (source, target) in enumerate(
-        ((weights_hbm, weights), (shift_hbm, shift), (mixing_hbm, mixing_out)))]
-    for copy in copies:
+    per_row = block // 6
+    copies = {}
+    number = 0
+    for which, (source, target) in enumerate(((signal_hbm, signal), (cotangent_hbm, cotangent))):
+        for part in range(4):
+            span = pl.ds(part * channels // 4, channels // 4)
+            copies[which, part] = pltpu.make_async_copy(source.at[span], target.at[span], arrived.at[number])
+            number += 1
+    for which, (source, target) in enumerate(((weights_hbm, weights), (shift_hbm, shift), (mixing_hbm, mixing))):
+        copies[2 + which, 0] = pltpu.make_async_copy(source, target, arrived.at[number])
+        number += 1
+    for copy in copies.values():
         copy.start()
-    widen_all(signal, cotangent, weights, wide, lambda which, _: copies[0].wait() if which == 2 else None)
-    copies[1].wait()
+    widen_all(signal, cotangent, weights, wide, lambda *key: copies[key].wait())
+    copies[3, 0].wait()
+    copies[4, 0].wait()
+    order = mixing.shape[0]
+    rest = jnp.zeros((channels, 2 * LANES - order * channels), BF16)
+    for i in range(2):
+        tiles = [mixing[k] if i else mixing[k].astype(F32).T.astype(BF16) for k in range(order)]
+        matrix = side_by_side(tiles + [rest])
+        rows_out[rows // per_row, i] = jnp.concatenate(
+            [matrix[:, :LANES], matrix[:, LANES:], jnp.zeros((PACKED - 2 * channels, LANES), BF16)], axis=0)
+    for i in range(2, EXTRA):
+        rows_out[rows // per_row, i] = jnp.zeros((PACKED, LANES), BF16)
     load_row = row_loader(channels, rows, shift, wide)
     selector = strip_selector()
-    size = 6
-
-    def each(i, _):
-        strips = []
-        for j in range(size):
-            s = i * size + j
-            tiles = [load_row(block * b + s) for b in range(BLOCKS)]
+    lane = lane_index((PACKED, LANES))
+
+    def sends(t):
+        return [pltpu.make_async_copy(source, target, sent.at[t, i]) for i, (source, target) in enumerate((
+            (west_out.at[t], west_hbm.at[t]), (east_out.at[t], east_hbm.at[t]),
+            (strips_out.at[:, t], strips_hbm.at[:, t]), (rows_out.at[:, t], rows_hbm.at[:, t])))]
+
+    def each(t, _):
+        groups = []
+        for m in range(6):
+            tiles = [load_row(block * b + per_row * m + t) for b in range(BLOCKS)]
             for b in range(BLOCKS):
-                rows_out[block * b + s] = tiles[b]
-            strips.append(side_by_side(tiles))
-        strips = jnp.dot(jnp.concatenate(strips, axis=0), selector, preferred_element_type=F32).astype(BF16)
-        for j in range(size):
-            strips_out[i * size + j] = strips[PACKED * j:PACKED * (j + 1)]
+                rows_out[b * 6 + m, t] = tiles[b]
+            groups.append(side_by_side(tiles))
+        strips = jnp.dot(jnp.concatenate(groups, axis=0), selector, preferred_element_type=F32).astype(BF16)
+        west = jnp.zeros((PACKED, LANES), BF16)
+        east = jnp.zeros((PACKED, LANES), BF16)
+        for m in range(6):
+            strip = strips[PACKED * m:PACKED * (m + 1)]
+            strips_out[m, t] = strip
+            west = jnp.where((lane - 5 * m - 5) % GROUP < 5, turned(strip, 5 * m), west)
+            east = jnp.where((lane - 5 * m) % GROUP < 5, turned(strip, 5 * m - SIDE - 6), east)
+        west_out[t] = west
+        east_out[t] = east
+        for copy in sends(t):
+            copy.start()
         return 0
 
-    lax.fori_loop(0, block // size, each, 0)
-    copies[2].wait()
-
-
-def merge_kernel(strips_in, rows_in, from_west, from_east, strips_out, north_out, south_out):
+    lax.fori_loop(0, per_row, each, 0)
+    for t in range(per_row):
+        for copy in sends(t):
+            copy.wait()
+
+
+def merge_kernel(strips_in, rows_in, from_west, from_east, _, strips_out, north_out, south_out):
     block = strips_in.shape[0]
-    rows = rows_in.shape[0]
+    rows = rows_in.shape[0] - EXTRA
     per_row = block // 6
     lane = lane_index((PACKED, LANES))
     lane_in = lane % GROUP
@@ -267,11 +270,11 @@
 
 
 class Chain:
-    def __init__(self, first, other, mixing, guards, scratch):
+    def __init__(self, first, other, order, rows_in, guards, scratch):
         self.buffers, self.kept, self.coef, self.wide = scratch[:3], *scratch[3:6]
         self.paired = scratch[6] if other is not None else None
-        self.first, self.other, self.mixing = first, other, mixing
-        self.order, self.channels = mixing.shape[:2]
+        self.first, self.other, self.rows_in, self.order = first, other, rows_in, order
+        self.channels = self.buffers[0].shape[1]
         self.total = self.kept.shape[0]
         for begin, end in guards:
             for index in range(begin, end):
@@ -292,19 +295,13 @@
         if self.other is not None:
             self.paired[index] = part(self.other, self.channels)
 
-    def put_all(self, index, ref, unroll):
-        count = ref.shape[0]
-
-        def several(i, _):
-            for j in range(unroll):
-                self.put(index + i * unroll + j, ref, i * unroll + j)
-            return 0
-
-        lax.fori_loop(0, count // unroll, several, 0)
+    def put_some(self, index, ref, first, count):
+        for i in range(count):
+            self.put(index + i, ref, first + i)
 
     def put_strips(self, strips, north, south):
         block = strips.shape[0]
-        self.put_all(1 + HALO, strips, block)
+        self.put_some(1 + HALO, strips, 0, block)
         lane = lane_index((PACKED, LANES))
         for i in range(HALO):
             at_end = i == HALO - 1
@@ -331,12 +328,10 @@
         return side_by_side([self.kept[i] for i in indices])
 
     def mixed(self, terms):
-        if self.other is not None:
-            matrix = self.mixing[...].reshape(self.order * self.channels, self.channels)
-            value = lax.dot_general(matrix, terms, CONTRACT_ROWS, preferred_element_type=F32)
-        else:
-            matrix = side_by_side([self.mixing[k] for k in range(self.order)])
-            value = jnp.dot(matrix, terms, preferred_element_type=F32)
+        place = self.rows_in.shape[0] - EXTRA + (self.other is None)
+        matrix = side_by_side([self.rows_in[place, i:i + self.channels, :] for i in (0, self.channels)])
+        matrix = matrix[:, :self.order * self.channels]
+        value = jnp.dot(matrix, terms, preferred_element_type=F32)
         return value.astype(BF16)
 
     def paired_with(self, indices, valid, terms):
@@ -351,48 +346,36 @@
     return (lane >= HALO) & (lane < LANES - HALO), in_strips
 
 
-def main_forward(rows_in, mixing, out, grad, *scratch):
-    rows = rows_in.shape[0]
-    order, channels = mixing.shape[:2]
-    chain = Chain(0, channels, mixing, ((0, 1), (rows + 1, rows + 8)), scratch)
-    chain.put_all(1, rows_in, rows // 2)
-    chain.run(2, ((0, rows),))
+def main_forward(upper, order, rows_in, _, out, grad, *scratch):
+    rows = rows_in.shape[0] - EXTRA
+    channels = out.shape[1]
+    half = rows // 2
+    count = half + HALO
+    chain = Chain(0, channels, order, rows_in, ((0, 1), (count + 1, count + 4)), scratch)
+    chain.put_some(1, rows_in, 0 if upper else half - HALO, count)
+    chain.run(1, ((0, count),))
     valid, _ = valid_lanes(channels)
-
-    def products(start, count, total_grad):
-        indices = [start + 1 + i for i in range(count)]
-        terms = chain.terms(indices)
-        value = chain.mixed(terms)
-        for i in range(count):
-            out[start + i] = value[:, LANES * i:LANES * (i + 1)]
-        return total_grad + chain.paired_with(indices, valid, terms)
-
-    inner = rows - 2 * HALO
-    total_grad = jnp.zeros(grad.shape, F32)
-    half = inner // 2
-    grad[...] = lax.fori_loop(0, 2, lambda i, g: products(HALO + i * half, half, g), total_grad)
-
-
-def main_backward(is_last, rows_in, north, south, mixing, summed, out, summed_out, *scratch):
-    rows = rows_in.shape[0]
-    channels = mixing.shape[1]
-    count = rows + 2 * HALO
-    chain = Chain(channels, None, mixing, ((0, 1), (count + 1, scratch[0].shape[0])), scratch)
-    for i in range(HALO):
-        chain.put(1 + i, north, i)
-        chain.put(1 + HALO + rows + i, south, i)
-    chain.put_all(1 + HALO, rows_in, rows // 2)
-    chain.run(2, ((0, count),), (is_last[0] == 1, lambda row, lane: row == HALO + rows))
-
+    indices = [1 + HALO + i for i in range(half - HALO)]
+    terms = chain.terms(indices)
+    value = chain.mixed(terms)
+    for i in range(len(indices)):
+        out[i + HALO * upper] = value[:, LANES * i:LANES * (i + 1)]
+    grad[...] = chain.paired_with(indices, valid, terms)
+
+
+def main_backward(upper, order, is_last, rows_in, beyond, summed, out, summed_out, *scratch):
+    rows = rows_in.shape[0] - EXTRA
+    channels = out.shape[1]
     half = rows // 2
-
-    def products(i, _):
-        value = chain.mixed(chain.terms([1 + HALO + i * half + j for j in range(half)]))
-        for j in range(half):
-            out[i * half + j] = value[:, LANES * j:LANES * (j + 1)]
-        return 0
-
-    lax.fori_loop(0, 2, products, 0)
+    count = half + 2 * HALO
+    chain = Chain(channels, None, order, rows_in, ((0, 1), (count + 1, count + 4)), scratch)
+    chain.put_some(1 if upper else 1 + HALO + half, beyond, 0, HALO)
+    chain.put_some(1 + HALO * upper, rows_in, 0 if upper else half - HALO, half + HALO)
+    closed = None if upper else (is_last[0] == 1, lambda row, lane: row == HALO + half)
+    chain.run(1, ((0, count),), closed)
+    value = chain.mixed(chain.terms([1 + HALO + i for i in range(half)]))
+    for i in range(half):
+        out[i] = value[:, LANES * i:LANES * (i + 1)]
     summed_out[...] = summed[...]
 
 
@@ -404,12 +387,12 @@
     return block, top, bottom, -(-(bottom + BAND + 5) // 8) * 8
 
 
-def edge_forward(is_last, strips_in, rows_in, north, south, mixing, out, grad, *scratch):
-    rows = rows_in.shape[0]
+def edge_forward(order, is_last, strips_in, rows_in, north, south, out, grad, *scratch):
+    rows = rows_in.shape[0] - EXTRA
     block, top, bottom, total = edge_sizes(rows)
-    channels = mixing.shape[1]
+    channels = out.shape[1]
     count = block + 2 * HALO
-    chain = Chain(0, channels, mixing, ((0, 1), (1 + count, top + 1), (top + 1 + BAND, bottom + 1),
+    chain = Chain(0, channels, order, rows_in, ((0, 1), (1 + count, top + 1), (top + 1 + BAND, bottom + 1),
                                         (bottom + 1 + BAND, total)), scratch)
     chain.put_strips(strips_in, north, south)
     for i in range(HALO):
@@ -438,10 +421,10 @@
     grad[...] = total_grad
 
 
-def edge_backward(is_last, strips_in, north, south, mixing, summed, out, summed_out, *scratch):
+def edge_backward(order, is_last, strips_in, rows_in, north, south, summed, out, summed_out, *scratch):
     block = strips_in.shape[0]
     count = block + 2 * HALO
-    chain = Chain(mixing.shape[1], None, mixing, ((0, 1), (1 + count, scratch[0].shape[0])), scratch)
+    chain = Chain(out.shape[1], None, order, rows_in, ((0, 1), (1 + count, scratch[0].shape[0])), scratch)
     chain.put_strips(strips_in, north, south)
     chain.run(1, ((0, count),), (is_last[0] == 1, lambda row, lane: (row == HALO + block) & (lane >= LANES - GROUP)))
     value = chain.mixed(chain.terms([1 + HALO + i for i in range(block)]))
@@ -450,9 +433,10 @@
     summed_out[...] = summed[...]
 
 
-def assemble_kernel(main, edges, summed, out_hbm, summed_out, wide, out, sent):
+def assemble_kernel(upper, lower, edges, summed, out_hbm, summed_out, wide, out, sent):
     summed_out[...] = summed[...]
-    rows, channels, _ = main.shape
+    half, channels, _ = upper.shape
+    rows = 2 * half
     block = rows // BLOCKS
     lane = lane_index((channels, LANES))
 
@@ -465,7 +449,8 @@
 
     for b in range(BLOCKS):
         for s in range(block):
-            put(block * b + s, s, b, main[block * b + s])
+            r = block * b + s
+            put(r, s, b, upper[r] if r < half else lower[r - half])
     if edges.shape[0] > block:
         for i in range(HALO):
             put(i, i, 0, edges[block + i])
@@ -511,63 +496,44 @@
     def weighs(mib):
         return pl.CostEstimate(flops=0, bytes_accessed=mib * 1024 * 1024, transcendentals=0)
 
-    all_wide = pltpu.VMEM((spread_size(2 * channels + 8, rows), LANES), F32)
-    raw = (signal, cotangent, edge_weights, circle_shift)
-    to_west, to_east = pl.pallas_call(
-        pack_kernel,
-        out_shape=(packed(block // 6), packed(block // 6)),
-        in_specs=[hbm, hbm, hbm, smem],
-        out_specs=(vmem, vmem),
+    per_row = block // 6
+    to_west, to_east, own_strips, rows_in = pl.pallas_call(
+        head_kernel,
+        out_shape=(packed(per_row), packed(per_row), shape((6, per_row, PACKED, LANES), BF16),
+                   shape((rows // per_row + 1, per_row, PACKED, LANES), BF16)),
+        in_specs=[hbm] * 5,
+        out_specs=(hbm,) * 4,
         scratch_shapes=[
             pltpu.VMEM(signal.shape, BF16),
             pltpu.VMEM(signal.shape, BF16),
             pltpu.VMEM(edge_weights.shape, BF16),
-            all_wide,
-            pltpu.SemaphoreType.DMA((9,)),
+            pltpu.SMEM(circle_shift.shape, jnp.int32),
+            pltpu.VMEM(mixing.shape, BF16),
+            pltpu.VMEM((spread_size(2 * channels + 8, rows), LANES), F32),
+            pltpu.VMEM((per_row, PACKED, LANES), BF16),
+            pltpu.VMEM((per_row, PACKED, LANES), BF16),
+            pltpu.VMEM((6, per_row, PACKED, LANES), BF16),
+            pltpu.VMEM((rows // per_row + 1, per_row, PACKED, LANES), BF16),
+            pltpu.SemaphoreType.DMA((11,)),
+            pltpu.SemaphoreType.DMA((per_row, 4)),
         ],
         compiler_params=pltpu.CompilerParams(vmem_limit_bytes=PACK_VMEM),
-        name="pack",
-    )(*raw)
+        name="head",
+    )(signal, cotangent, edge_weights, circle_shift, mixing)
+    own_strips = own_strips.reshape(block, PACKED, LANES)
+    rows_in = rows_in.reshape(rows + EXTRA, PACKED, LANES)
 
     eastward = [(i, (i + 1) % lon) for i in range(lon)]
     westward = [(j, i) for i, j in eastward]
     from_west = lax.ppermute(to_east, "lon", eastward)
     from_east = lax.ppermute(to_west, "lon", westward)
 
-    own_strips, rows_in, mixing = pl.pallas_call(
-        own_kernel,
-        out_shape=(packed(block), packed(rows), shape(mixing.shape, BF16)),
-        in_specs=[vmem, vmem, hbm, hbm, hbm],
-        out_specs=(vmem, vmem, vmem),
-        scratch_shapes=[
-            all_wide,
-            pltpu.VMEM(edge_weights.shape, BF16),
-            pltpu.SMEM(circle_shift.shape, jnp.int32),
-            pltpu.SemaphoreType.DMA((3,)),
-        ],
-        compiler_params=params(20),
-        cost_estimate=weighs(8),
-        name="own",
-    )(*raw, mixing)
-
-    strips, to_north, to_south = pl.pallas_call(
-        merge_kernel,
-        out_shape=(packed(block), packed(HALO + 2), packed(HALO + 2)),
-        in_specs=[vmem] * 4,
-        out_specs=(vmem,) * 3,
-        compiler_params=params(8),
-        name="merge",
-    )(own_strips, rows_in, from_west, from_east)
-
-    southward = [(i, i + 1) for i in range(lat - 1)]
-    northward = [(j, i) for i, j in southward]
-    north = lax.ppermute(to_south, "lat", southward)
-    south = lax.ppermute(to_north, "lat", northward)
-
-    rows_first = shape((rows, channels, LANES), BF16)
+    half = rows // 2
+    half_shape = shape((half, channels, LANES), BF16)
     grad_shape = shape((channels, order * channels), F32)
 
     def chain_scratch(total, with_pairs):
+        total = -(-total // 8) * 8
         scratch = [pltpu.VMEM((total, channels, LANES), F32)] * 3 + [
             pltpu.VMEM((total, order * channels, LANES), BF16),
             pltpu.VMEM((7 * total, LANES), F32),
@@ -575,28 +541,47 @@
         ]
         return scratch + [pltpu.VMEM((total, channels, LANES), BF16)] * with_pairs
 
-    main_f, grad_main = pl.pallas_call(
-        main_forward,
-        out_shape=(rows_first, grad_shape),
-        in_specs=[vmem, vmem],
-        out_specs=(vmem, vmem),
-        scratch_shapes=chain_scratch(rows + 8, True),
-        compiler_params=params(20),
-        cost_estimate=weighs(24),
-        name="main_forward",
-    )(rows_in, mixing)
+    def run_main_forward(upper, after):
+        return pl.pallas_call(
+            functools.partial(main_forward, upper, order),
+            out_shape=(half_shape, grad_shape),
+            in_specs=[vmem, vmem],
+            out_specs=(vmem, vmem),
+            scratch_shapes=chain_scratch(half + HALO + 4, True),
+            compiler_params=params(16),
+            cost_estimate=weighs(12),
+            name="forward_upper" if upper else "forward_lower",
+        )(rows_in, after)
+
+    upper_f, grad_upper = run_main_forward(True, rows_in)
+
+    strips, to_north, to_south = pl.pallas_call(
+        merge_kernel,
+        out_shape=(packed(block), packed(HALO + 2), packed(HALO + 2)),
+        in_specs=[vmem] * 5,
+        out_specs=(vmem,) * 3,
+        compiler_params=params(8),
+        name="merge",
+    )(own_strips, rows_in, from_west, from_east, grad_upper)
+
+    southward = [(i, i + 1) for i in range(lat - 1)]
+    northward = [(j, i) for i, j in southward]
+    north = lax.ppermute(to_south, "lat", southward)
+    south = lax.ppermute(to_north, "lat", northward)
+
+    lower_f, grad_lower = run_main_forward(False, to_north)
 
     is_last = (lax.axis_index("lat") == lat - 1).astype(jnp.int32).reshape(1)
     edge_f, grad_edge = pl.pallas_call(
-        edge_forward,
+        functools.partial(edge_forward, order),
         out_shape=(shape((block + 2 * HALO, channels, LANES), BF16), grad_shape),
-        in_specs=[smem] + [vmem] * 5,
+        in_specs=[smem] + [vmem] * 4,
         out_specs=(vmem, vmem),
         scratch_shapes=chain_scratch(edge_total, True),
         compiler_params=params(16),
         cost_estimate=weighs(12),
         name="edge_forward",
-    )(is_last, strips, rows_in, north, south, mixing)
+    )(is_last, strips, rows_in, north, south)
 
     rounds = []
     for axis, devices in (("lon", lon), ("lat", lat)):
@@ -608,37 +593,38 @@
 
     results = {}
 
-    def run_main_backward(share):
-        results["main"], share = pl.pallas_call(
-            main_backward,
-            out_shape=(rows_first, grad_shape),
-            in_specs=[smem] + [vmem] * 5,
+    def run_backward_half(upper, share):
+        name = "backward_upper" if upper else "backward_lower"
+        results[name], share = pl.pallas_call(
+            functools.partial(main_backward, upper, order),
+            out_shape=(half_shape, grad_shape),
+            in_specs=[smem] + [vmem] * 3,
             out_specs=(vmem, vmem),
-            scratch_shapes=chain_scratch(-(-(rows + 2 * HALO + 8) // 8) * 8, False),
-            compiler_params=params(20),
-            cost_estimate=weighs(24),
-            name="main_backward",
-        )(is_last, rows_in, north, south, mixing, share)
+            scratch_shapes=chain_scratch(half + 2 * HALO + 4, False),
+            compiler_params=params(16),
+            cost_estimate=weighs(12),
+            name=name,
+        )(is_last, rows_in, north if upper else south, share)
         return share
 
     def run_edge_backward(share):
         results["edge"], share = pl.pallas_call(
-            edge_backward,
+            functools.partial(edge_backward, order),
             out_shape=(shape((block, channels, LANES), BF16), grad_shape),
             in_specs=[smem] + [vmem] * 5,
             out_specs=(vmem, vmem),
-            scratch_shapes=chain_scratch(-(-(block + 2 * HALO + 8) // 8) * 8, False),
+            scratch_shapes=chain_scratch(block + 2 * HALO + 8, False),
             compiler_params=params(12),
             cost_estimate=weighs(12),
             name="edge_backward",
-        )(is_last, strips, north, south, mixing, share)
+        )(is_last, strips, rows_in, north, south, share)
         return share
 
-    def assemble(main, edges, share, name):
+    def assemble(upper, lower, edges, share, name):
         return pl.pallas_call(
             assemble_kernel,
             out_shape=(shape(signal.shape, BF16), grad_shape),
-            in_specs=[vmem] * 3,
+            in_specs=[vmem] * 4,
             out_specs=(hbm, vmem),
             scratch_shapes=[
                 pltpu.VMEM((spread_size(channels, rows), LANES), F32),
@@ -648,18 +634,20 @@
             compiler_params=params(12),
             cost_estimate=weighs(8),
             name=name,
-        )(main, edges, share)
+        )(upper, lower, edges, share)
 
     def run_assemble_forward(share):
-        results["output"], share = assemble(main_f, edge_f, share, "assemble_forward")
+        results["output"], share = assemble(upper_f, lower_f, edge_f, share, "assemble_forward")
         return share
 
     def run_assemble_backward(share):
-        results["signal_grad"], share = assemble(results["main"], results["edge"], share, "assemble_backward")
+        results["signal_grad"], share = assemble(
+            results["backward_upper"], results["backward_lower"], results["edge"], share, "assemble_backward")
         return share
 
-    beside = [run_main_backward, run_assemble_forward, run_edge_backward, run_assemble_backward]
-    share = grad_main + grad_edge
+    beside = [functools.partial(run_backward_half, True), functools.partial(run_backward_half, False), run_edge_backward,
+              run_assemble_forward, run_assemble_backward]
+    share = grad_upper + grad_lower + grad_edge
     theirs = jnp.zeros_like(share)
     for number in range(max(len(rounds), len(beside))):
         if number:

time: 55.5 us -> 48.5 us (0.87)
  Pallas kernels: 30.6 us -> 27.5 us
  local copies, waits for them, and re-layouts: 3.15 us -> 1.58 us
  starting transfers between devices: 17.4 us -> 16.2 us
  waiting for transfers between devices: 2.87 us -> 2.05 us
    pallas_call x6 -> x7, Pallas kernels: 26.3 us -> 23.3 us  [the longest x2 7.04 us: run_main_forward(): pl.pallas_call(functools.partial(main_forward, upper, order), out_shape=(...]
    unnamed x14 -> x6, local copies, waits for them, and re-layouts: 3.15 us -> 1.58 us
    ppermute x5, waiting for transfers between devices: 2.83 us -> 1.3 us  [on_device(): lax.ppermute(share, *rounds[number])]
    ppermute x5, starting transfers between devices: 6.12 us -> 4.77 us  [on_device(): lax.ppermute(share, *rounds[number])]
    ppermute x1, waiting for transfers between devices: 0.01 us -> 0.75 us  [on_device(): south = lax.ppermute(to_north, 'lat', northward)]
  transfers between devices with their start and end apart: 9 -> 9, of which waited for: 3 -> 2; matrix products, arithmetic and copies ran while one was open for 0% -> 0% of each run, Pallas kernels for 40% -> 38%
where the time goes in v1:
time: 48.5 us; the launch traced here: 48.3 us
  Pallas kernels  27.5 us (57%)
  starting transfers between devices  16.2 us (33%)
  waiting for transfers between devices  2.05 us (4%)
  local copies, waits for them, and re-layouts  1.58 us (3%)
  between operations  0.87 us (2%)
    pallas_call x2, Pallas kernels, run_main_forward(): pl.pallas_call(functools.partial(main_forward, upper, order), out_shape=(...  7.04 us
    pallas_call x2, Pallas kernels, run_backward_half(): pl.pallas_call(functools.partial(main_backward, upper, order), out_shape=...  6.5 us
    ppermute x5, starting transfers between devices, on_device(): lax.ppermute(share, *rounds[number])  4.77 us
    pallas_call x1, Pallas kernels, on_device(): pl.pallas_call(head_kernel, out_shape=(packed(per_row), packed(per_row),...  4.37 us
    ppermute x1, starting transfers between devices, on_device(): north = lax.ppermute(to_south, 'lat', southward)  4.12 us
    pallas_call x1, Pallas kernels, on_device(): pl.pallas_call(functools.partial(edge_forward, order), out_shape=(shape((...  3.5 us
    ppermute x1, starting transfers between devices, on_device(): from_east = lax.ppermute(to_west, 'lon', westward)  3.1 us
    pallas_call x2, Pallas kernels, assemble(): pl.pallas_call(assemble_kernel, out_shape=(shape(signal.shape, BF16), gra...  2.87 us
  transfers between devices with their start and end apart: 9, of which 2 were waited for; matrix products, arithmetic and copies ran while one was open for 0% of the time, Pallas kernels for 38%

profile of v1, /device:TPU:1, one launch (start us, length us, event | category | flops | bytes accessed | tf_op | source)
XLA Modules:
  0.0 48.3 jit_solution(16738783267796328531)
XLA Ops:
  0.6 4.4 %head.1 = (bf16[4,80,128]{2,1,0:T(8,128)(2,1)}, bf16[4,80,128]{2,1,0:T(8,128)(2,1)}, bf16[6,4,80,128]{3,2,1,0:T(8,128)(2,1)}, bf16[25,4,80,128]{3,2,1,0:T(8,128)(2,1)}) custom-call(bf16[32,96,128]{2,1,0:T(8,128)(2,1)} %signal_hbm.1, bf16[32,96,128]{2,1,0:T(8,128)(2,1)} %cotangent_hbm.1, bf16[3,96,128]{2,1,0:T(8,128)(2,1)} %weights_hbm.1, s32[96]{0:T(128)} %shift_hbm.1, ...), custom_call_target="tpu_custom_call" | custom-call | tf_op jit(solution)/shard_map/head/pallas_call | solution.py:500
  5.0 2.1 %collective-permute-start = (bf16[4,80,128]{2,1,0:T(8,128)(2,1)}, bf16[4,80,128]{2,1,0:T(8,128)(2,1)S(1)}, u32[]{:S(2)}, u32[]{:S(2)}) collective-permute-start(bf16[4,80,128]{2,1,0:T(8,128)(2,1)} %get-tuple-element.29), channel_id=1, source_target_pairs={{0,1},{1,2},{2,3},{3,4},{4,5},{5,6},{6,7},{7,0},{8,9},{9,10},{10,1... | collective-permute-start | bytes 245768 | tf_op jit(solution)/shard_map/ppermute | solution.py:528
  7.1 3.1 %collective-permute-start.1 = (bf16[4,80,128]{2,1,0:T(8,128)(2,1)}, bf16[4,80,128]{2,1,0:T(8,128)(2,1)S(1)}, u32[]{:S(2)}, u32[]{:S(2)}) collective-permute-start(bf16[4,80,128]{2,1,0:T(8,128)(2,1)} %get-tuple-element.30), channel_id=1, source_target_pairs={{1,0},{2,1},{3,2},{4,3},{5,4},{6,5},{7,6},{0,7},{9,8},{10,9},{11,1... | collective-permute-start | bytes 245768 | tf_op jit(solution)/shard_map/ppermute | solution.py:529
  10.2 1.6 %copy-done = bf16[25,4,80,128]{3,2,1,0:T(8,128)(2,1)S(1)} copy-done((bf16[25,4,80,128]{3,2,1,0:T(8,128)(2,1)S(1)}, bf16[25,4,80,128]{3,2,1,0:T(8,128)(2,1)}, u32[]{:S(2)}) %copy-start) | copy-done | bytes 2048024
  11.8 3.5 %forward_upper.1 = (bf16[48,32,128]{2,1,0:T(8,128)(2,1)S(1)}, f32[32,192]{1,0:T(8,128)S(1)}) custom-call(bf16[100,80,128]{2,1,0:T(8,128)(2,1)S(1)} %bitcast.3, bf16[100,80,128]{2,1,0:T(8,128)(2,1)S(1)} %bitcast.4), custom_call_target="tpu_custom_call" | custom-call | bytes 12582912 | tf_op jit(solution)/shard_map/forward_upper/pallas_call | solution.py:545
  15.3 0.0 collective-permute-done.1.from_east
  15.4 0.6 %merge.1 = (bf16[24,80,128]{2,1,0:T(8,128)(2,1)S(1)}, bf16[7,80,128]{2,1,0:T(8,128)(2,1)S(1)}, bf16[7,80,128]{2,1,0:T(8,128)(2,1)S(1)}) custom-call(bf16[24,80,128]{2,1,0:T(8,128)(2,1)S(1)} %bitcast.11, bf16[100,80,128]{2,1,0:T(8,128)(2,1)S(1)} %bitcast.5, bf16[4,80,128]{2,1,0:T(8,128)(2,1)S(1)} %collective-permute-done.from_west, ...), custom_call_target="tpu_custom_call" | custom-call | tf_op jit(solution)/shard_map/merge/pallas_call | solution.py:558
  16.0 4.1 %collective-permute-start.2 = (bf16[7,80,128]{2,1,0:T(8,128)(2,1)S(1)}, bf16[7,80,128]{2,1,0:T(8,128)(2,1)S(1)}, u32[]{:S(2)}, u32[]{:S(2)}) collective-permute-start(bf16[7,80,128]{2,1,0:T(8,128)(2,1)S(1)} %get-tuple-element.35), channel_id=1, source_target_pairs={{0,8},{8,16},{16,24},{1,9},{9,17},{17,25},{2,10},{10,18},{18,26},{... | collective-permute-start | bytes 430088 | tf_op jit(solution)/shard_map/ppermute | solution.py:569
  20.1 2.1 %collective-permute-start.3 = (bf16[7,80,128]{2,1,0:T(8,128)(2,1)S(1)}, bf16[7,80,128]{2,1,0:T(8,128)(2,1)S(1)}, u32[]{:S(2)}, u32[]{:S(2)}) collective-permute-start(bf16[7,80,128]{2,1,0:T(8,128)(2,1)S(1)} %get-tuple-element.32._), channel_id=1, source_target_pairs={{8,0},{16,8},{24,16},{9,1},{17,9},{25,17},{10,2},{18,10},{26,18},{... | collective-permute-start | bytes 430088 | tf_op jit(solution)/shard_map/ppermute | solution.py:570
  22.2 3.5 %forward_lower.1 = (bf16[48,32,128]{2,1,0:T(8,128)(2,1)S(1)}, f32[32,192]{1,0:T(8,128)S(1)}) custom-call(bf16[100,80,128]{2,1,0:T(8,128)(2,1)S(1)} %bitcast.6, bf16[7,80,128]{2,1,0:T(8,128)(2,1)S(1)} %get-tuple-element.32._), custom_call_target="tpu_custom_call" | custom-call | bytes 12582912 | tf_op jit(solution)/shard_map/forward_lower/pallas_call | solution.py:545
  25.8 0.8 %collective-permute-done.3.south.beyond = bf16[7,80,128]{2,1,0:T(8,128)(2,1)S(1)} collective-permute-done((bf16[7,80,128]{2,1,0:T(8,128)(2,1)S(1)}, bf16[7,80,128]{2,1,0:T(8,128)(2,1)S(1)}, u32[]{:S(2)}, u32[]{:S(2)}) %collective-permute-start.3) | collective-permute-done | bytes 143392 | tf_op jit(solution)/shard_map/ppermute | solution.py:570
  26.5 3.5 %edge_forward.1 = (bf16[34,32,128]{2,1,0:T(8,128)(2,1)S(1)}, f32[32,192]{1,0:T(8,128)S(1)}) custom-call(s32[1]{0:T(128)} %bitcast.2.is_last, bf16[24,80,128]{2,1,0:T(8,128)(2,1)S(1)} %get-tuple-element.34.strips_in, bf16[100,80,128]{2,1,0:T(8,128)(2,1)S(1)} %bitcast.7, bf16[7,80,128]{2,1,0:T(8,128)(2,1)S(1)} %collective-permute-done.2.north.beyond, ...), custom_call_target="tpu_custom_call" | custom-call | bytes 12582912 | tf_op jit(solution)/shard_map/edge_forward/pallas_call | solution.py:575
  30.1 0.1 collective-permute-start.4
  30.2 3.1 %backward_upper.1 = (bf16[48,32,128]{2,1,0:T(8,128)(2,1)S(1)}, f32[32,192]{1,0:T(8,128)S(1)}) custom-call(s32[1]{0:T(128)} %bitcast.2.is_last, bf16[100,80,128]{2,1,0:T(8,128)(2,1)S(1)} %bitcast.8, bf16[7,80,128]{2,1,0:T(8,128)(2,1)S(1)} %collective-permute-done.2.north.beyond, f32[32,192]{1,0:T(8,128)S(1)} %add_add_fusion.summed), custom_call_target="tpu_custom_call" | custom-call | bytes 12582912 | tf_op jit(solution)/shard_map/backward_upper/pallas_call | solution.py:598
  33.3 0.1 collective-permute-start.5
  33.4 3.4 %backward_lower.1 = (bf16[48,32,128]{2,1,0:T(8,128)(2,1)S(1)}, f32[32,192]{1,0:T(8,128)S(1)}) custom-call(s32[1]{0:T(128)} %bitcast.2.is_last, bf16[100,80,128]{2,1,0:T(8,128)(2,1)S(1)} %bitcast.9, bf16[7,80,128]{2,1,0:T(8,128)(2,1)S(1)} %collective-permute-done.3.south.beyond, f32[32,192]{1,0:T(8,128)S(1)} %add.20.summed), custom_call_target="tpu_custom_call" | custom-call | bytes 12582912 | tf_op jit(solution)/shard_map/backward_lower/pallas_call | solution.py:598
  36.8 2.5 %collective-permute-start.6 = (f32[32,192]{1,0:T(8,128)S(1)}, f32[32,192]{1,0:T(8,128)S(1)}, u32[]{:S(2)}, u32[]{:S(2)}) collective-permute-start(f32[32,192]{1,0:T(8,128)S(1)} %add.21.summed), channel_id=1, source_target_pairs={{0,4},{1,5},{2,6},{3,7},{4,0},{5,1},{6,2},{7,3},{8,12},{9,13},{10,... | collective-permute-start | bytes 73736 | tf_op jit(solution)/shard_map/ppermute | solution.py:655
  39.3 1.9 %edge_backward.1 = (bf16[24,32,128]{2,1,0:T(8,128)(2,1)S(1)}, f32[32,192]{1,0:T(8,128)S(1)}) custom-call(s32[1]{0:T(128)} %bitcast.2.is_last, bf16[24,80,128]{2,1,0:T(8,128)(2,1)S(1)} %get-tuple-element.34.strips_in, bf16[100,80,128]{2,1,0:T(8,128)(2,1)S(1)} %bitcast.10, bf16[7,80,128]{2,1,0:T(8,128)(2,1)S(1)} %collective-permute-done.2.north.beyond, ...), custom_call_target="tpu_custom_call" | custom-call | bytes 12582912 | tf_op jit(solution)/shard_map/edge_backward/pallas_call | solution.py:611
  41.2 0.1 collective-permute-start.7
  41.3 1.5 %assemble_forward.1 = (bf16[32,96,128]{2,1,0:T(8,128)(2,1)}, f32[32,192]{1,0:T(8,128)S(1)}) custom-call(bf16[48,32,128]{2,1,0:T(8,128)(2,1)S(1)} %get-tuple-element.27.upper, bf16[48,32,128]{2,1,0:T(8,128)(2,1)S(1)} %get-tuple-element.33.lower, bf16[34,32,128]{2,1,0:T(8,128)(2,1)S(1)} %get-tuple-element.36.edges, f32[32,192]{1,0:T(8,128)S(1)} %add.22.summed), custom_call_target="tpu_custom_call" | custom-call | bytes 8388608 | tf_op jit(solution)/shard_map/assemble_forward/pallas_call | solution.py:624
  42.8 1.3 %collective-permute-done.7 = f32[32,192]{1,0:T(8,128)S(1)} collective-permute-done((f32[32,192]{1,0:T(8,128)S(1)}, f32[32,192]{1,0:T(8,128)S(1)}, u32[]{:S(2)}, u32[]{:S(2)}) %collective-permute-start.7) | collective-permute-done | bytes 24608 | tf_op jit(solution)/shard_map/ppermute | solution.py:655
  44.1 2.0 %collective-permute-start.8 = (f32[32,192]{1,0:T(8,128)S(1)}, f32[32,192]{1,0:T(8,128)S(1)}, u32[]{:S(2)}, u32[]{:S(2)}) collective-permute-start(f32[32,192]{1,0:T(8,128)S(1)} %add.23.summed), channel_id=1, source_target_pairs={{0,8},{8,0},{16,24},{24,16},{1,9},{9,1},{17,25},{25,17},{2,10},{10... | collective-permute-start | bytes 73736 | tf_op jit(solution)/shard_map/ppermute | solution.py:655
  46.1 1.4 %assemble_backward.1 = (bf16[32,96,128]{2,1,0:T(8,128)(2,1)}, f32[32,192]{1,0:T(8,128)S(1)}) custom-call(bf16[48,32,128]{2,1,0:T(8,128)(2,1)S(1)} %get-tuple-element.43.upper, bf16[48,32,128]{2,1,0:T(8,128)(2,1)S(1)} %get-tuple-element.44.lower, bf16[24,32,128]{2,1,0:T(8,128)(2,1)S(1)} %get-tuple-element.45.edges, f32[32,192]{1,0:T(8,128)S(1)} %add.23.summed), custom_call_target="tpu_custom_call" | custom-call | bytes 8388608 | tf_op jit(solution)/shard_map/assemble_backward/pallas_call | solution.py:624
  47.5 0.7 %finish.1 = f32[6,32,32]{2,1,0:T(8,128)} custom-call(f32[32,192]{1,0:T(8,128)S(1)} %get-tuple-element.48.mine, f32[32,192]{1,0:T(8,128)S(1)} %collective-permute-done.8.theirs), custom_call_target="tpu_custom_call" | custom-call | tf_op jit(solution)/shard_map/finish/pallas_call | solution.py:660
  (16 shorter events, 0.1 us)
Async XLA Ops:
  5.0 10.3 %collective-permute-start = (bf16[4,80,128]{2,1,0:T(8,128)(2,1)}, bf16[4,80,128]{2,1,0:T(8,128)(2,1)S(1)}, u32[]{:S(2)}, u32[]{:S(2)}) collective-permute-start(bf16[4,80,128]{2,1,0:T(8,128)(2,1)} %get-tuple-element.29), channel_id=1, source_target_pairs={{0,1},{1,2},{2,3},{3,4},{4,5},{5,6},{6,7},{7,0},{8,9},{9,10},{10,1... | collective-permute-start | bytes 245768 | tf_op jit(solution)/shard_map/ppermute | solution.py:528
  7.1 8.2 %collective-permute-start.1 = (bf16[4,80,128]{2,1,0:T(8,128)(2,1)}, bf16[4,80,128]{2,1,0:T(8,128)(2,1)S(1)}, u32[]{:S(2)}, u32[]{:S(2)}) collective-permute-start(bf16[4,80,128]{2,1,0:T(8,128)(2,1)} %get-tuple-element.30), channel_id=1, source_target_pairs={{1,0},{2,1},{3,2},{4,3},{5,4},{6,5},{7,6},{0,7},{9,8},{10,9},{11,1... | collective-permute-start | bytes 245768 | tf_op jit(solution)/shard_map/ppermute | solution.py:529
  10.2 1.6 %copy-start = (bf16[25,4,80,128]{3,2,1,0:T(8,128)(2,1)S(1)}, bf16[25,4,80,128]{3,2,1,0:T(8,128)(2,1)}, u32[]{:S(2)}) copy-start(bf16[25,4,80,128]{3,2,1,0:T(8,128)(2,1)} %get-tuple-element.26) | copy-start | bytes 6144004
  11.8 3.6 %copy-start.2 = (bf16[6,4,80,128]{3,2,1,0:T(8,128)(2,1)S(1)}, bf16[6,4,80,128]{3,2,1,0:T(8,128)(2,1)}, u32[]{:S(2)}) copy-start(bf16[6,4,80,128]{3,2,1,0:T(8,128)(2,1)} %get-tuple-element.28) | copy-start | bytes 1474564
  15.3 6.9 %copy-start.1 = (bf16[25,4,80,128]{3,2,1,0:T(8,128)(2,1)S(1)}, bf16[25,4,80,128]{3,2,1,0:T(8,128)(2,1)}, u32[]{:S(2)}) copy-start(bf16[25,4,80,128]{3,2,1,0:T(8,128)(2,1)} %get-tuple-element.26) | copy-start | bytes 6144004
  16.0 9.8 %collective-permute-start.2 = (bf16[7,80,128]{2,1,0:T(8,128)(2,1)S(1)}, bf16[7,80,128]{2,1,0:T(8,128)(2,1)S(1)}, u32[]{:S(2)}, u32[]{:S(2)}) collective-permute-start(bf16[7,80,128]{2,1,0:T(8,128)(2,1)S(1)} %get-tuple-element.35), channel_id=1, source_target_pairs={{0,8},{8,16},{16,24},{1,9},{9,17},{17,25},{2,10},{10,18},{18,26},{... | collective-permute-start | bytes 430088 | tf_op jit(solution)/shard_map/ppermute | solution.py:569
  20.1 6.4 %collective-permute-start.3 = (bf16[7,80,128]{2,1,0:T(8,128)(2,1)S(1)}, bf16[7,80,128]{2,1,0:T(8,128)(2,1)S(1)}, u32[]{:S(2)}, u32[]{:S(2)}) collective-permute-start(bf16[7,80,128]{2,1,0:T(8,128)(2,1)S(1)} %get-tuple-element.32._), channel_id=1, source_target_pairs={{8,0},{16,8},{24,16},{9,1},{17,9},{25,17},{10,2},{18,10},{26,18},{... | collective-permute-start | bytes 430088 | tf_op jit(solution)/shard_map/ppermute | solution.py:570
  30.1 3.2 %collective-permute-start.4 = (f32[32,192]{1,0:T(8,128)S(1)}, f32[32,192]{1,0:T(8,128)S(1)}, u32[]{:S(2)}, u32[]{:S(2)}) collective-permute-start(f32[32,192]{1,0:T(8,128)S(1)} %add_add_fusion.summed), channel_id=1, source_target_pairs={{0,1},{1,0},{2,3},{3,2},{4,5},{5,4},{6,7},{7,6},{8,9},{9,8},{10,11... | collective-permute-start | bytes 73736 | tf_op jit(solution)/shard_map/ppermute | solution.py:655
  33.3 3.4 %collective-permute-start.5 = (f32[32,192]{1,0:T(8,128)S(1)}, f32[32,192]{1,0:T(8,128)S(1)}, u32[]{:S(2)}, u32[]{:S(2)}) collective-permute-start(f32[32,192]{1,0:T(8,128)S(1)} %add.20.summed), channel_id=1, source_target_pairs={{0,2},{1,3},{2,0},{3,1},{4,6},{5,7},{6,4},{7,5},{8,10},{9,11},{10,... | collective-permute-start | bytes 73736 | tf_op jit(solution)/shard_map/ppermute | solution.py:655
  36.8 4.4 %collective-permute-start.6 = (f32[32,192]{1,0:T(8,128)S(1)}, f32[32,192]{1,0:T(8,128)S(1)}, u32[]{:S(2)}, u32[]{:S(2)}) collective-permute-start(f32[32,192]{1,0:T(8,128)S(1)} %add.21.summed), channel_id=1, source_target_pairs={{0,4},{1,5},{2,6},{3,7},{4,0},{5,1},{6,2},{7,3},{8,12},{9,13},{10,... | collective-permute-start | bytes 73736 | tf_op jit(solution)/shard_map/ppermute | solution.py:655
  41.2 2.8 %collective-permute-start.7 = (f32[32,192]{1,0:T(8,128)S(1)}, f32[32,192]{1,0:T(8,128)S(1)}, u32[]{:S(2)}, u32[]{:S(2)}) collective-permute-start(f32[32,192]{1,0:T(8,128)S(1)} %add.22.summed), channel_id=1, source_target_pairs={{0,16},{8,24},{16,0},{24,8},{1,17},{9,25},{17,1},{25,9},{2,18},{10... | collective-permute-start | bytes 73736 | tf_op jit(solution)/shard_map/ppermute | solution.py:655
  44.1 3.5 %collective-permute-start.8 = (f32[32,192]{1,0:T(8,128)S(1)}, f32[32,192]{1,0:T(8,128)S(1)}, u32[]{:S(2)}, u32[]{:S(2)}) collective-permute-start(f32[32,192]{1,0:T(8,128)S(1)} %add.23.summed), channel_id=1, source_target_pairs={{0,8},{8,0},{16,24},{24,16},{1,9},{9,1},{17,25},{25,17},{2,10},{10... | collective-permute-start | bytes 73736 | tf_op jit(solution)/shard_map/ppermute | solution.py:655

commit v2 on v1

--- a/solution.py
+++ b/solution.py
@@ -87,8 +87,22 @@
 EXTRA = 4
 
 
-def head_kernel(signal_hbm, cotangent_hbm, weights_hbm, shift_hbm, mixing_hbm, west_hbm, east_hbm, strips_hbm, rows_hbm,
-                signal, cotangent, weights, shift, mixing, wide, west_out, east_out, strips_out, rows_out, arrived, sent):
+def flags(place):
+    return [(place[0] >> i) & 1 == 1 for i in range(3)]
+
+
+class Either:
+    def __init__(self, flag, yes, no):
+        self.flag, self.yes, self.no = flag, yes, no
+
+    def __getitem__(self, key):
+        return jnp.where(self.flag, self.yes[key], self.no[key])
+
+
+def head_kernel(place, signal_hbm, cotangent_hbm, weights_hbm, shift_hbm, mixing_hbm,
+                first_hbm, second_hbm, strips_hbm, upper_hbm, lower_hbm,
+                signal, cotangent, weights, shift, mixing, wide, first_out, second_out, strips_out, rows_out, arrived, sent):
+    odd = flags(place)[1]
     channels, rows, _ = signal.shape
     block = rows // BLOCKS
     per_row = block // 6
@@ -120,10 +134,17 @@
     selector = strip_selector()
     lane = lane_index((PACKED, LANES))
 
+    units = rows // per_row
+    near = upper_hbm.shape[0] - 1
+
     def sends(t):
-        return [pltpu.make_async_copy(source, target, sent.at[t, i]) for i, (source, target) in enumerate((
-            (west_out.at[t], west_hbm.at[t]), (east_out.at[t], east_hbm.at[t]),
-            (strips_out.at[:, t], strips_hbm.at[:, t]), (rows_out.at[:, t], rows_hbm.at[:, t])))]
+        pairs = (
+            (first_out.at[t], first_hbm.at[t]), (second_out.at[t], second_hbm.at[t]),
+            (strips_out.at[:, t], strips_hbm.at[:, t]),
+            (rows_out.at[pl.ds(0, near), t], upper_hbm.at[pl.ds(0, near), t]),
+            (rows_out.at[pl.ds(units, 1), t], upper_hbm.at[pl.ds(near, 1), t]),
+            (rows_out.at[pl.ds(units - near, near + 1), t], lower_hbm.at[:, t]))
+        return [pltpu.make_async_copy(*pair, sent.at[t, i]) for i, pair in enumerate(pairs)]
 
     def each(t, _):
         groups = []
@@ -140,8 +161,8 @@
             strips_out[m, t] = strip
             west = jnp.where((lane - 5 * m - 5) % GROUP < 5, turned(strip, 5 * m), west)
             east = jnp.where((lane - 5 * m) % GROUP < 5, turned(strip, 5 * m - SIDE - 6), east)
-        west_out[t] = west
-        east_out[t] = east
+        first_out[t] = jnp.where(odd, west, east)
+        second_out[t] = jnp.where(odd, east, west)
         for copy in sends(t):
             copy.start()
         return 0
@@ -152,9 +173,12 @@
             copy.wait()
 
 
-def merge_kernel(strips_in, rows_in, from_west, from_east, _, strips_out, north_out, south_out):
+def merge_kernel(place, strips_in, upper, lower, lon_first, lon_second, _, strips_out, first_out, second_out):
     block = strips_in.shape[0]
-    rows = rows_in.shape[0] - EXTRA
+    near = upper.shape[0] - EXTRA
+    _, odd, odd_lat = flags(place)
+    from_west = Either(odd, lon_first, lon_second)
+    from_east = Either(odd, lon_second, lon_first)
     per_row = block // 6
     lane = lane_index((PACKED, LANES))
     lane_in = lane % GROUP
@@ -170,16 +194,20 @@
         return 0
 
     lax.fori_loop(0, per_row, each, 0)
-    for out, first_row, first_strip, side in (
-        (north_out, 0, 0, 0), (south_out, rows - HALO, block - HALO, BLOCKS - 1)):
+    to_north, to_south = [], []
+    for out, rows_in, first_row, first_strip, side in (
+        (to_north, upper, 0, 0, 0), (to_south, lower, near - HALO, block - HALO, BLOCKS - 1)):
         for i in range(HALO):
-            out[i] = rows_in[first_row + i]
+            out.append(rows_in[first_row + i])
         corner = turned(strips_out[first_strip], -GROUP * side)
         for g in range(1, BLOCKS):
             piece = turned(strips_out[first_strip + g], GROUP * (g - side))
             corner = jnp.where((lane >= GROUP * g) & (lane < GROUP * (g + 1)), piece, corner)
-        out[HALO] = corner
-        out[HALO + 1] = turned(strips_out[first_strip + HALO - 1], -GROUP * side)
+        out.append(corner)
+        out.append(turned(strips_out[first_strip + HALO - 1], -GROUP * side))
+    for i in range(HALO + 2):
+        first_out[i] = jnp.where(odd_lat, to_north[i], to_south[i])
+        second_out[i] = jnp.where(odd_lat, to_south[i], to_north[i])
 
 
 def write_coefficients(total, first, w_east, w_south, w_diag, parity, keep, coef, shifted):
@@ -347,12 +375,12 @@
 
 
 def main_forward(upper, order, rows_in, _, out, grad, *scratch):
-    rows = rows_in.shape[0] - EXTRA
     channels = out.shape[1]
-    half = rows // 2
+    half = out.shape[0]
     count = half + HALO
+    near = rows_in.shape[0] - EXTRA
     chain = Chain(0, channels, order, rows_in, ((0, 1), (count + 1, count + 4)), scratch)
-    chain.put_some(1, rows_in, 0 if upper else half - HALO, count)
+    chain.put_some(1, rows_in, 0 if upper else near - count, count)
     chain.run(1, ((0, count),))
     valid, _ = valid_lanes(channels)
     indices = [1 + HALO + i for i in range(half - HALO)]
@@ -363,15 +391,17 @@
     grad[...] = chain.paired_with(indices, valid, terms)
 
 
-def main_backward(upper, order, is_last, rows_in, beyond, summed, out, summed_out, *scratch):
-    rows = rows_in.shape[0] - EXTRA
+def main_backward(upper, order, place, rows_in, lat_first, lat_second, summed, out, summed_out, *scratch):
     channels = out.shape[1]
-    half = rows // 2
+    half = out.shape[0]
     count = half + 2 * HALO
+    near = rows_in.shape[0] - EXTRA
+    is_last, _, odd = flags(place)
+    beyond = Either(odd, lat_first, lat_second) if upper else Either(odd, lat_second, lat_first)
     chain = Chain(channels, None, order, rows_in, ((0, 1), (count + 1, count + 4)), scratch)
     chain.put_some(1 if upper else 1 + HALO + half, beyond, 0, HALO)
-    chain.put_some(1 + HALO * upper, rows_in, 0 if upper else half - HALO, half + HALO)
-    closed = None if upper else (is_last[0] == 1, lambda row, lane: row == HALO + half)
+    chain.put_some(1 + HALO * upper, rows_in, 0 if upper else near - half - HALO, half + HALO)
+    closed = None if upper else (is_last, lambda row, lane: row == HALO + half)
     chain.run(1, ((0, count),), closed)
     value = chain.mixed(chain.terms([1 + HALO + i for i in range(half)]))
     for i in range(half):
@@ -387,9 +417,11 @@
     return block, top, bottom, -(-(bottom + BAND + 5) // 8) * 8
 
 
-def edge_forward(order, is_last, strips_in, rows_in, north, south, out, grad, *scratch):
-    rows = rows_in.shape[0] - EXTRA
-    block, top, bottom, total = edge_sizes(rows)
+def edge_forward(order, place, strips_in, rows_in, lower, lat_first, lat_second, out, grad, *scratch):
+    near = rows_in.shape[0] - EXTRA
+    block, top, bottom, total = edge_sizes(strips_in.shape[0] * BLOCKS)
+    is_last, _, odd = flags(place)
+    north, south = Either(odd, lat_first, lat_second), Either(odd, lat_second, lat_first)
     channels = out.shape[1]
     count = block + 2 * HALO
     chain = Chain(0, channels, order, rows_in, ((0, 1), (1 + count, top + 1), (top + 1 + BAND, bottom + 1),
@@ -400,12 +432,12 @@
         chain.put(bottom + 1 + 2 * HALO + i, south, i)
     for i in range(2 * HALO):
         chain.put(top + 1 + HALO + i, rows_in, i)
-        chain.put(bottom + 1 + i, rows_in, rows - 2 * HALO + i)
+        chain.put(bottom + 1 + i, lower, near - 2 * HALO + i)
 
     def closed(row, lane):
         return (row == bottom + 2 * HALO) | ((row == HALO + block) & (lane >= LANES - GROUP))
 
-    chain.run(1, ((0, count), (top, BAND), (bottom, BAND)), (is_last[0] == 1, closed))
+    chain.run(1, ((0, count), (top, BAND), (bottom, BAND)), (is_last, closed))
     main_valid, strip_valid = valid_lanes(channels)
     strip_rows = [1 + HALO + i for i in range(block)]
     band_rows = [top + 1 + HALO + i for i in range(HALO)] + [bottom + 1 + HALO + i for i in range(HALO)]
@@ -421,12 +453,14 @@
     grad[...] = total_grad
 
 
-def edge_backward(order, is_last, strips_in, rows_in, north, south, summed, out, summed_out, *scratch):
+def edge_backward(order, place, strips_in, rows_in, lat_first, lat_second, summed, out, summed_out, *scratch):
     block = strips_in.shape[0]
+    is_last, _, odd = flags(place)
+    north, south = Either(odd, lat_first, lat_second), Either(odd, lat_second, lat_first)
     count = block + 2 * HALO
     chain = Chain(out.shape[1], None, order, rows_in, ((0, 1), (1 + count, scratch[0].shape[0])), scratch)
     chain.put_strips(strips_in, north, south)
-    chain.run(1, ((0, count),), (is_last[0] == 1, lambda row, lane: (row == HALO + block) & (lane >= LANES - GROUP)))
+    chain.run(1, ((0, count),), (is_last, lambda row, lane: (row == HALO + block) & (lane >= LANES - GROUP)))
     value = chain.mixed(chain.terms([1 + HALO + i for i in range(block)]))
     for i in range(block):
         out[i] = value[:, LANES * i:LANES * (i + 1)]
@@ -497,12 +531,17 @@
         return pl.CostEstimate(flops=0, bytes_accessed=mib * 1024 * 1024, transcendentals=0)
 
     per_row = block // 6
-    to_west, to_east, own_strips, rows_in = pl.pallas_call(
+    half = rows // 2
+    near = -(-(half + HALO) // per_row)
+    half_rows = shape((near + 1, per_row, PACKED, LANES), BF16)
+    at_lat, at_lon = lax.axis_index("lat"), lax.axis_index("lon")
+    place = (at_lat == lat - 1).astype(jnp.int32) + 2 * (at_lon % 2) + 4 * (at_lat % 2)
+    place = place.astype(jnp.int32).reshape(1)
+    lon_first, lon_second, own_strips, upper, lower = pl.pallas_call(
         head_kernel,
-        out_shape=(packed(per_row), packed(per_row), shape((6, per_row, PACKED, LANES), BF16),
-                   shape((rows // per_row + 1, per_row, PACKED, LANES), BF16)),
-        in_specs=[hbm] * 5,
-        out_specs=(hbm,) * 4,
+        out_shape=(packed(per_row), packed(per_row), shape((6, per_row, PACKED, LANES), BF16), half_rows, half_rows),
+        in_specs=[smem] + [hbm] * 5,
+        out_specs=(hbm,) * 5,
         scratch_shapes=[
             pltpu.VMEM(signal.shape, BF16),
             pltpu.VMEM(signal.shape, BF16),
@@ -515,20 +554,19 @@
             pltpu.VMEM((6, per_row, PACKED, LANES), BF16),
             pltpu.VMEM((rows // per_row + 1, per_row, PACKED, LANES), BF16),
             pltpu.SemaphoreType.DMA((11,)),
-            pltpu.SemaphoreType.DMA((per_row, 4)),
+            pltpu.SemaphoreType.DMA((per_row, 6)),
         ],
         compiler_params=pltpu.CompilerParams(vmem_limit_bytes=PACK_VMEM),
         name="head",
-    )(signal, cotangent, edge_weights, circle_shift, mixing)
+    )(place, signal, cotangent, edge_weights, circle_shift, mixing)
     own_strips = own_strips.reshape(block, PACKED, LANES)
-    rows_in = rows_in.reshape(rows + EXTRA, PACKED, LANES)
-
-    eastward = [(i, (i + 1) % lon) for i in range(lon)]
-    westward = [(j, i) for i, j in eastward]
-    from_west = lax.ppermute(to_east, "lon", eastward)
-    from_east = lax.ppermute(to_west, "lon", westward)
-
-    half = rows // 2
+    upper, lower = [array.reshape((near + 1) * per_row, PACKED, LANES) for array in (upper, lower)]
+
+    pairs = [(i, i ^ 1) for i in range(lon)]
+    other_pairs = [(i, (i + 1 if i % 2 else i - 1) % lon) for i in range(lon)]
+    lon_first = lax.ppermute(lon_first, "lon", pairs)
+    lon_second = lax.ppermute(lon_second, "lon", other_pairs)
+
     half_shape = shape((half, channels, LANES), BF16)
     grad_shape = shape((channels, order * channels), F32)
 
@@ -541,47 +579,46 @@
         ]
         return scratch + [pltpu.VMEM((total, channels, LANES), BF16)] * with_pairs
 
-    def run_main_forward(upper, after):
+    def run_main_forward(is_upper, after):
         return pl.pallas_call(
-            functools.partial(main_forward, upper, order),
+            functools.partial(main_forward, is_upper, order),
             out_shape=(half_shape, grad_shape),
             in_specs=[vmem, vmem],
             out_specs=(vmem, vmem),
             scratch_shapes=chain_scratch(half + HALO + 4, True),
             compiler_params=params(16),
             cost_estimate=weighs(12),
-            name="forward_upper" if upper else "forward_lower",
-        )(rows_in, after)
-
-    upper_f, grad_upper = run_main_forward(True, rows_in)
-
-    strips, to_north, to_south = pl.pallas_call(
+            name="forward_upper" if is_upper else "forward_lower",
+        )(upper if is_upper else lower, after)
+
+    upper_f, grad_upper = run_main_forward(True, upper)
+
+    strips, lat_first, lat_second = pl.pallas_call(
         merge_kernel,
         out_shape=(packed(block), packed(HALO + 2), packed(HALO + 2)),
-        in_specs=[vmem] * 5,
+        in_specs=[smem] + [vmem] * 6,
         out_specs=(vmem,) * 3,
         compiler_params=params(8),
         name="merge",
-    )(own_strips, rows_in, from_west, from_east, grad_upper)
-
-    southward = [(i, i + 1) for i in range(lat - 1)]
-    northward = [(j, i) for i, j in southward]
-    north = lax.ppermute(to_south, "lat", southward)
-    south = lax.ppermute(to_north, "lat", northward)
-
-    lower_f, grad_lower = run_main_forward(False, to_north)
-
-    is_last = (lax.axis_index("lat") == lat - 1).astype(jnp.int32).reshape(1)
+    )(place, own_strips, upper, lower, lon_first, lon_second, grad_upper)
+
+    pairs = [(i, i ^ 1) for i in range(lat)]
+    other_pairs = [(i, i + 1 if i % 2 else i - 1) for i in range(1, lat - 1)]
+    after = lat_first
+    lat_first = lax.ppermute(lat_first, "lat", pairs)
+    lat_second = lax.ppermute(lat_second, "lat", other_pairs)
+    lower_f, grad_lower = run_main_forward(False, after)
+
     edge_f, grad_edge = pl.pallas_call(
         functools.partial(edge_forward, order),
         out_shape=(shape((block + 2 * HALO, channels, LANES), BF16), grad_shape),
-        in_specs=[smem] + [vmem] * 4,
+        in_specs=[smem] + [vmem] * 5,
         out_specs=(vmem, vmem),
         scratch_shapes=chain_scratch(edge_total, True),
         compiler_params=params(16),
         cost_estimate=weighs(12),
         name="edge_forward",
-    )(is_last, strips, rows_in, north, south)
+    )(place, strips, upper, lower, lat_first, lat_second)
 
     rounds = []
     for axis, devices in (("lon", lon), ("lat", lat)):
@@ -593,18 +630,18 @@
 
     results = {}
 
-    def run_backward_half(upper, share):
-        name = "backward_upper" if upper else "backward_lower"
+    def run_backward_half(is_upper, share):
+        name = "backward_upper" if is_upper else "backward_lower"
         results[name], share = pl.pallas_call(
-            functools.partial(main_backward, upper, order),
+            functools.partial(main_backward, is_upper, order),
             out_shape=(half_shape, grad_shape),
-            in_specs=[smem] + [vmem] * 3,
+            in_specs=[smem] + [vmem] * 4,
             out_specs=(vmem, vmem),
             scratch_shapes=chain_scratch(half + 2 * HALO + 4, False),
             compiler_params=params(16),
             cost_estimate=weighs(12),
             name=name,
-        )(is_last, rows_in, north if upper else south, share)
+        )(place, upper if is_upper else lower, lat_first, lat_second, share)
         return share
 
     def run_edge_backward(share):
@@ -617,7 +654,7 @@
             compiler_params=params(12),
             cost_estimate=weighs(12),
             name="edge_backward",
-        )(is_last, strips, rows_in, north, south, share)
+        )(place, strips, upper, lat_first, lat_second, share)
         return share
 
     def assemble(upper, lower, edges, share, name):

time: 48.5 us -> 47.4 us (0.977)
  waiting for transfers between devices: 2.05 us -> 1.21 us
    ppermute x4, starting transfers between devices: 11.4 us -> 10 us  [the longest x1 4.58 us: on_device(): lat_second = lax.ppermute(lat_second, 'lat', other_pairs)]
    ppermute x5, starting transfers between devices: 4.77 us -> 5.91 us  [on_device(): lax.ppermute(share, *rounds[number])]
    ppermute x4, waiting for transfers between devices: 0.76 us -> 0.01 us  [the longest x1 0.01 us: on_device(): lat_first = lax.ppermute(lat_first, 'lat', pairs)]
    unnamed x6 -> x8, local copies, waits for them, and re-layouts: 1.58 us -> 1.3 us
  transfers between devices with their start and end apart: 9 -> 9, of which waited for: 2 -> 1; matrix products, arithmetic and copies ran while one was open for 0% -> 0% of each run, Pallas kernels for 38% -> 39%
where the time goes in v2:
time: 47.4 us; the launch traced here: 47.2 us
  Pallas kernels  27.8 us (59%)
  starting transfers between devices  16 us (34%)
  local copies, waits for them, and re-layouts  1.3 us (3%)
  waiting for transfers between devices  1.21 us (3%)
  between operations  0.89 us (2%)
    pallas_call x2, Pallas kernels, run_main_forward(): pl.pallas_call(functools.partial(main_forward, is_upper, order), out_shap...  7.07 us
    pallas_call x2, Pallas kernels, run_backward_half(): pl.pallas_call(functools.partial(main_backward, is_upper, order), out_sha...  6.57 us
    ppermute x5, starting transfers between devices, on_device(): lax.ppermute(share, *rounds[number])  5.91 us
    ppermute x1, starting transfers between devices, on_device(): lat_second = lax.ppermute(lat_second, 'lat', other_pairs)  4.58 us
    pallas_call x1, Pallas kernels, on_device(): pl.pallas_call(head_kernel, out_shape=(packed(per_row), packed(per_row),...  4.47 us
    pallas_call x1, Pallas kernels, on_device(): pl.pallas_call(functools.partial(edge_forward, order), out_shape=(shape((...  3.52 us
    ppermute x1, starting transfers between devices, on_device(): lon_second = lax.ppermute(lon_second, 'lon', other_pairs)  3.29 us
    pallas_call x2, Pallas kernels, assemble(): pl.pallas_call(assemble_kernel, out_shape=(shape(signal.shape, BF16), gra...  2.87 us
  transfers between devices with their start and end apart: 9, of which 1 were waited for; matrix products, arithmetic and copies ran while one was open for 0% of the time, Pallas kernels for 39%

profile of v2, /device:TPU:1, one launch (start us, length us, event | category | flops | bytes accessed | tf_op | source)
XLA Modules:
  0.0 47.2 jit_solution(4921327363146957010)
XLA Ops:
  0.7 4.5 %head.1 = (bf16[4,80,128]{2,1,0:T(8,128)(2,1)}, bf16[4,80,128]{2,1,0:T(8,128)(2,1)}, bf16[6,4,80,128]{3,2,1,0:T(8,128)(2,1)}, bf16[15,4,80,128]{3,2,1,0:T(8,128)(2,1)}, bf16[15,4,80,128]{3,2,1,0:T(8,128)(2,1)}) custom-call(s32[1]{0:T(128)} %bitcast.place, bf16[32,96,128]{2,1,0:T(8,128)(2,1)} %signal_hbm.1, bf16[32,96,128]{2,1,0:T(8,128)(2,1)} %cotangent_hbm.1, ...), custom_call_target="tpu_custom_call" | custom-call | tf_op jit(solution)/shard_map/head/pallas_call | solution.py:540
  5.1 2.1 %collective-permute-start = (bf16[4,80,128]{2,1,0:T(8,128)(2,1)}, bf16[4,80,128]{2,1,0:T(8,128)(2,1)S(1)}, u32[]{:S(2)}, u32[]{:S(2)}) collective-permute-start(bf16[4,80,128]{2,1,0:T(8,128)(2,1)} %get-tuple-element.31), channel_id=1, source_target_pairs={{0,1},{1,0},{2,3},{3,2},{4,5},{5,4},{6,7},{7,6},{8,9},{9,8},{10,11... | collective-permute-start | bytes 245768 | tf_op jit(solution)/shard_map/ppermute | solution.py:567
  7.2 3.3 %collective-permute-start.1 = (bf16[4,80,128]{2,1,0:T(8,128)(2,1)}, bf16[4,80,128]{2,1,0:T(8,128)(2,1)S(1)}, u32[]{:S(2)}, u32[]{:S(2)}) collective-permute-start(bf16[4,80,128]{2,1,0:T(8,128)(2,1)} %get-tuple-element.32), channel_id=1, source_target_pairs={{0,7},{1,2},{2,1},{3,4},{4,3},{5,6},{6,5},{7,0},{8,15},{9,10},{10,... | collective-permute-start | bytes 245768 | tf_op jit(solution)/shard_map/ppermute | solution.py:568
  10.5 1.3 %copy-done = bf16[15,4,80,128]{3,2,1,0:T(8,128)(2,1)S(1)} copy-done((bf16[15,4,80,128]{3,2,1,0:T(8,128)(2,1)S(1)}, bf16[15,4,80,128]{3,2,1,0:T(8,128)(2,1)}, u32[]{:S(2)}) %copy-start) | copy-done | bytes 1228824
  11.8 3.5 %forward_upper.1 = (bf16[48,32,128]{2,1,0:T(8,128)(2,1)S(1)}, f32[32,192]{1,0:T(8,128)S(1)}) custom-call(bf16[60,80,128]{2,1,0:T(8,128)(2,1)S(1)} %bitcast.4, bf16[60,80,128]{2,1,0:T(8,128)(2,1)S(1)} %bitcast.5), custom_call_target="tpu_custom_call" | custom-call | bytes 12582912 | tf_op jit(solution)/shard_map/forward_upper/pallas_call | solution.py:583
  15.4 0.6 %merge.1 = (bf16[24,80,128]{2,1,0:T(8,128)(2,1)S(1)}, bf16[7,80,128]{2,1,0:T(8,128)(2,1)S(1)}, bf16[7,80,128]{2,1,0:T(8,128)(2,1)S(1)}) custom-call(s32[1]{0:T(128)} %bitcast.place, bf16[24,80,128]{2,1,0:T(8,128)(2,1)S(1)} %bitcast.14, bf16[60,80,128]{2,1,0:T(8,128)(2,1)S(1)} %bitcast.6, bf16[60,80,128]{2,1,0:T(8,128)(2,1)S(1)} %bitcast.10, ...), custom_call_target="tpu_custom_call" | custom-call | tf_op jit(solution)/shard_map/merge/pallas_call | solution.py:596
  16.1 4.6 %collective-permute-start.3 = (bf16[7,80,128]{2,1,0:T(8,128)(2,1)S(1)}, bf16[7,80,128]{2,1,0:T(8,128)(2,1)S(1)}, u32[]{:S(2)}, u32[]{:S(2)}) collective-permute-start(bf16[7,80,128]{2,1,0:T(8,128)(2,1)S(1)} %get-tuple-element.37), channel_id=1, source_target_pairs={{8,16},{16,8},{9,17},{17,9},{10,18},{18,10},{11,19},{19,11},{12,20... | collective-permute-start | bytes 430088 | tf_op jit(solution)/shard_map/ppermute | solution.py:609
  20.6 0.1 collective-permute-start.2
  20.7 3.5 %forward_lower.1 = (bf16[48,32,128]{2,1,0:T(8,128)(2,1)S(1)}, f32[32,192]{1,0:T(8,128)S(1)}) custom-call(bf16[60,80,128]{2,1,0:T(8,128)(2,1)S(1)} %bitcast.11, bf16[7,80,128]{2,1,0:T(8,128)(2,1)S(1)} %get-tuple-element.34._), custom_call_target="tpu_custom_call" | custom-call | bytes 12582912 | tf_op jit(solution)/shard_map/forward_lower/pallas_call | solution.py:583
  24.3 0.0 collective-permute-done.2.lat_first
  24.3 3.5 %edge_forward.1 = (bf16[34,32,128]{2,1,0:T(8,128)(2,1)S(1)}, f32[32,192]{1,0:T(8,128)S(1)}) custom-call(s32[1]{0:T(128)} %bitcast.place, bf16[24,80,128]{2,1,0:T(8,128)(2,1)S(1)} %get-tuple-element.36.strips_in, bf16[60,80,128]{2,1,0:T(8,128)(2,1)S(1)} %bitcast.7, bf16[60,80,128]{2,1,0:T(8,128)(2,1)S(1)} %bitcast.12, ...), custom_call_target="tpu_custom_call" | custom-call | bytes 12582912 | tf_op jit(solution)/shard_map/edge_forward/pallas_call | solution.py:612
  27.9 0.1 collective-permute-start.4
  28.0 3.2 %backward_upper.1 = (bf16[48,32,128]{2,1,0:T(8,128)(2,1)S(1)}, f32[32,192]{1,0:T(8,128)S(1)}) custom-call(s32[1]{0:T(128)} %bitcast.place, bf16[60,80,128]{2,1,0:T(8,128)(2,1)S(1)} %bitcast.8, bf16[7,80,128]{2,1,0:T(8,128)(2,1)S(1)} %collective-permute-done.2.lat_first, bf16[7,80,128]{2,1,0:T(8,128)(2,1)S(1)} %collective-permute-done.3.lat_second, ...), custom_call_target="tpu_custom_call" | custom-call | bytes 12582912 | tf_op jit(solution)/shard_map/backward_upper/pallas_call | solution.py:635
  31.2 0.5 %collective-permute-start.5 = (f32[32,192]{1,0:T(8,128)S(1)}, f32[32,192]{1,0:T(8,128)S(1)}, u32[]{:S(2)}, u32[]{:S(2)}) collective-permute-start(f32[32,192]{1,0:T(8,128)S(1)} %add.37.summed), channel_id=1, source_target_pairs={{0,2},{1,3},{2,0},{3,1},{4,6},{5,7},{6,4},{7,5},{8,10},{9,11},{10,... | collective-permute-start | bytes 73736 | tf_op jit(solution)/shard_map/ppermute | solution.py:692
  31.7 3.4 %backward_lower.1 = (bf16[48,32,128]{2,1,0:T(8,128)(2,1)S(1)}, f32[32,192]{1,0:T(8,128)S(1)}) custom-call(s32[1]{0:T(128)} %bitcast.place, bf16[60,80,128]{2,1,0:T(8,128)(2,1)S(1)} %bitcast.13, bf16[7,80,128]{2,1,0:T(8,128)(2,1)S(1)} %collective-permute-done.2.lat_first, bf16[7,80,128]{2,1,0:T(8,128)(2,1)S(1)} %collective-permute-done.3.lat_second, ...), custom_call_target="tpu_custom_call" | custom-call | bytes 12582912 | tf_op jit(solution)/shard_map/backward_lower/pallas_call | solution.py:635
  35.1 0.0 collective-permute-done.5
  35.1 2.4 %collective-permute-start.6 = (f32[32,192]{1,0:T(8,128)S(1)}, f32[32,192]{1,0:T(8,128)S(1)}, u32[]{:S(2)}, u32[]{:S(2)}) collective-permute-start(f32[32,192]{1,0:T(8,128)S(1)} %add.38.summed), channel_id=1, source_target_pairs={{0,4},{1,5},{2,6},{3,7},{4,0},{5,1},{6,2},{7,3},{8,12},{9,13},{10,... | collective-permute-start | bytes 73736 | tf_op jit(solution)/shard_map/ppermute | solution.py:692
  37.5 1.9 %edge_backward.1 = (bf16[24,32,128]{2,1,0:T(8,128)(2,1)S(1)}, f32[32,192]{1,0:T(8,128)S(1)}) custom-call(s32[1]{0:T(128)} %bitcast.place, bf16[24,80,128]{2,1,0:T(8,128)(2,1)S(1)} %get-tuple-element.36.strips_in, bf16[60,80,128]{2,1,0:T(8,128)(2,1)S(1)} %bitcast.9, bf16[7,80,128]{2,1,0:T(8,128)(2,1)S(1)} %collective-permute-done.2.lat_first, ...), custom_call_target="tpu_custom_call" | custom-call | bytes 12582912 | tf_op jit(solution)/shard_map/edge_backward/pallas_call | solution.py:648
  39.4 0.2 collective-permute-start.7
  39.6 1.5 %assemble_forward.1 = (bf16[32,96,128]{2,1,0:T(8,128)(2,1)}, f32[32,192]{1,0:T(8,128)S(1)}) custom-call(bf16[48,32,128]{2,1,0:T(8,128)(2,1)S(1)} %get-tuple-element.28.upper, bf16[48,32,128]{2,1,0:T(8,128)(2,1)S(1)} %get-tuple-element.35.lower, bf16[34,32,128]{2,1,0:T(8,128)(2,1)S(1)} %get-tuple-element.38.edges, f32[32,192]{1,0:T(8,128)S(1)} %add.39.summed), custom_call_target="tpu_custom_call" | custom-call | bytes 8388608 | tf_op jit(solution)/shard_map/assemble_forward/pallas_call | solution.py:661
  41.1 1.2 %collective-permute-done.7 = f32[32,192]{1,0:T(8,128)S(1)} collective-permute-done((f32[32,192]{1,0:T(8,128)S(1)}, f32[32,192]{1,0:T(8,128)S(1)}, u32[]{:S(2)}, u32[]{:S(2)}) %collective-permute-start.7) | collective-permute-done | bytes 24608 | tf_op jit(solution)/shard_map/ppermute | solution.py:692
  42.3 2.8 %collective-permute-start.8 = (f32[32,192]{1,0:T(8,128)S(1)}, f32[32,192]{1,0:T(8,128)S(1)}, u32[]{:S(2)}, u32[]{:S(2)}) collective-permute-start(f32[32,192]{1,0:T(8,128)S(1)} %add.40.summed), channel_id=1, source_target_pairs={{0,8},{8,0},{16,24},{24,16},{1,9},{9,1},{17,25},{25,17},{2,10},{10... | collective-permute-start | bytes 73736 | tf_op jit(solution)/shard_map/ppermute | solution.py:692
  45.0 1.4 %assemble_backward.1 = (bf16[32,96,128]{2,1,0:T(8,128)(2,1)}, f32[32,192]{1,0:T(8,128)S(1)}) custom-call(bf16[48,32,128]{2,1,0:T(8,128)(2,1)S(1)} %get-tuple-element.45.upper, bf16[48,32,128]{2,1,0:T(8,128)(2,1)S(1)} %get-tuple-element.46.lower, bf16[24,32,128]{2,1,0:T(8,128)(2,1)S(1)} %get-tuple-element.47.edges, f32[32,192]{1,0:T(8,128)S(1)} %add.40.summed), custom_call_target="tpu_custom_call" | custom-call | bytes 8388608 | tf_op jit(solution)/shard_map/assemble_backward/pallas_call | solution.py:661
  46.5 0.7 %finish.1 = f32[6,32,32]{2,1,0:T(8,128)} custom-call(f32[32,192]{1,0:T(8,128)S(1)} %get-tuple-element.50.mine, f32[32,192]{1,0:T(8,128)S(1)} %collective-permute-done.8.theirs), custom_call_target="tpu_custom_call" | custom-call | tf_op jit(solution)/shard_map/finish/pallas_call | solution.py:697
  (18 shorter events, 0.1 us)
Async XLA Ops:
  5.1 10.2 %collective-permute-start = (bf16[4,80,128]{2,1,0:T(8,128)(2,1)}, bf16[4,80,128]{2,1,0:T(8,128)(2,1)S(1)}, u32[]{:S(2)}, u32[]{:S(2)}) collective-permute-start(bf16[4,80,128]{2,1,0:T(8,128)(2,1)} %get-tuple-element.31), channel_id=1, source_target_pairs={{0,1},{1,0},{2,3},{3,2},{4,5},{5,4},{6,7},{7,6},{8,9},{9,8},{10,11... | collective-permute-start | bytes 245768 | tf_op jit(solution)/shard_map/ppermute | solution.py:567
  7.2 8.1 %collective-permute-start.1 = (bf16[4,80,128]{2,1,0:T(8,128)(2,1)}, bf16[4,80,128]{2,1,0:T(8,128)(2,1)S(1)}, u32[]{:S(2)}, u32[]{:S(2)}) collective-permute-start(bf16[4,80,128]{2,1,0:T(8,128)(2,1)} %get-tuple-element.32), channel_id=1, source_target_pairs={{0,7},{1,2},{2,1},{3,4},{4,3},{5,6},{6,5},{7,0},{8,15},{9,10},{10,... | collective-permute-start | bytes 245768 | tf_op jit(solution)/shard_map/ppermute | solution.py:568
  10.5 1.3 %copy-start = (bf16[15,4,80,128]{3,2,1,0:T(8,128)(2,1)S(1)}, bf16[15,4,80,128]{3,2,1,0:T(8,128)(2,1)}, u32[]{:S(2)}) copy-start(bf16[15,4,80,128]{3,2,1,0:T(8,128)(2,1)} %get-tuple-element.27) | copy-start | bytes 3686404
  11.8 3.6 %copy-start.2 = (bf16[15,4,80,128]{3,2,1,0:T(8,128)(2,1)S(1)}, bf16[15,4,80,128]{3,2,1,0:T(8,128)(2,1)}, u32[]{:S(2)}) copy-start(bf16[15,4,80,128]{3,2,1,0:T(8,128)(2,1)} %get-tuple-element.29) | copy-start | bytes 3686404
  11.8 3.6 %copy-start.3 = (bf16[6,4,80,128]{3,2,1,0:T(8,128)(2,1)S(1)}, bf16[6,4,80,128]{3,2,1,0:T(8,128)(2,1)}, u32[]{:S(2)}) copy-start(bf16[6,4,80,128]{3,2,1,0:T(8,128)(2,1)} %get-tuple-element.30) | copy-start | bytes 1474564
  16.0 8.3 %copy-start.1 = (bf16[15,4,80,128]{3,2,1,0:T(8,128)(2,1)S(1)}, bf16[15,4,80,128]{3,2,1,0:T(8,128)(2,1)}, u32[]{:S(2)}) copy-start(bf16[15,4,80,128]{3,2,1,0:T(8,128)(2,1)} %get-tuple-element.27) | copy-start | bytes 3686404
  16.1 8.2 %collective-permute-start.3 = (bf16[7,80,128]{2,1,0:T(8,128)(2,1)S(1)}, bf16[7,80,128]{2,1,0:T(8,128)(2,1)S(1)}, u32[]{:S(2)}, u32[]{:S(2)}) collective-permute-start(bf16[7,80,128]{2,1,0:T(8,128)(2,1)S(1)} %get-tuple-element.37), channel_id=1, source_target_pairs={{8,16},{16,8},{9,17},{17,9},{10,18},{18,10},{11,19},{19,11},{12,20... | collective-permute-start | bytes 430088 | tf_op jit(solution)/shard_map/ppermute | solution.py:609
  20.6 3.6 %collective-permute-start.2 = (bf16[7,80,128]{2,1,0:T(8,128)(2,1)S(1)}, bf16[7,80,128]{2,1,0:T(8,128)(2,1)S(1)}, u32[]{:S(2)}, u32[]{:S(2)}) collective-permute-start(bf16[7,80,128]{2,1,0:T(8,128)(2,1)S(1)} %get-tuple-element.34._), channel_id=1, source_target_pairs={{0,8},{8,0},{16,24},{24,16},{1,9},{9,1},{17,25},{25,17},{2,10},{10... | collective-permute-start | bytes 430088 | tf_op jit(solution)/shard_map/ppermute | solution.py:608
  27.9 3.3 %collective-permute-start.4 = (f32[32,192]{1,0:T(8,128)S(1)}, f32[32,192]{1,0:T(8,128)S(1)}, u32[]{:S(2)}, u32[]{:S(2)}) collective-permute-start(f32[32,192]{1,0:T(8,128)S(1)} %add_add_fusion.summed), channel_id=1, source_target_pairs={{0,1},{1,0},{2,3},{3,2},{4,5},{5,4},{6,7},{7,6},{8,9},{9,8},{10,11... | collective-permute-start | bytes 73736 | tf_op jit(solution)/shard_map/ppermute | solution.py:692
  31.2 3.9 %collective-permute-start.5 = (f32[32,192]{1,0:T(8,128)S(1)}, f32[32,192]{1,0:T(8,128)S(1)}, u32[]{:S(2)}, u32[]{:S(2)}) collective-permute-start(f32[32,192]{1,0:T(8,128)S(1)} %add.37.summed), channel_id=1, source_target_pairs={{0,2},{1,3},{2,0},{3,1},{4,6},{5,7},{6,4},{7,5},{8,10},{9,11},{10,... | collective-permute-start | bytes 73736 | tf_op jit(solution)/shard_map/ppermute | solution.py:692
  35.1 4.3 %collective-permute-start.6 = (f32[32,192]{1,0:T(8,128)S(1)}, f32[32,192]{1,0:T(8,128)S(1)}, u32[]{:S(2)}, u32[]{:S(2)}) collective-permute-start(f32[32,192]{1,0:T(8,128)S(1)} %add.38.summed), channel_id=1, source_target_pairs={{0,4},{1,5},{2,6},{3,7},{4,0},{5,1},{6,2},{7,3},{8,12},{9,13},{10,... | collective-permute-start | bytes 73736 | tf_op jit(solution)/shard_map/ppermute | solution.py:692
  39.4 2.8 %collective-permute-start.7 = (f32[32,192]{1,0:T(8,128)S(1)}, f32[32,192]{1,0:T(8,128)S(1)}, u32[]{:S(2)}, u32[]{:S(2)}) collective-permute-start(f32[32,192]{1,0:T(8,128)S(1)} %add.39.summed), channel_id=1, source_target_pairs={{0,16},{8,24},{16,0},{24,8},{1,17},{9,25},{17,1},{25,9},{2,18},{10... | collective-permute-start | bytes 73736 | tf_op jit(solution)/shard_map/ppermute | solution.py:692
  42.3 4.2 %collective-permute-start.8 = (f32[32,192]{1,0:T(8,128)S(1)}, f32[32,192]{1,0:T(8,128)S(1)}, u32[]{:S(2)}, u32[]{:S(2)}) collective-permute-start(f32[32,192]{1,0:T(8,128)S(1)} %add.40.summed), channel_id=1, source_target_pairs={{0,8},{8,0},{16,24},{24,16},{1,9},{9,1},{17,25},{25,17},{2,10},{10... | collective-permute-start | bytes 73736 | tf_op jit(solution)/shard_map/ppermute | solution.py:692

commit v3 on v2

--- a/solution.py
+++ b/solution.py
@@ -234,22 +234,27 @@
     def step(position, now, older, newer):
         last = position == order - 1
 
-        def one_row(at, level, down, before):
+        def one_row(at, level, down, before, has_new=True, has_level=True, has_down=True):
             coefs = [coef_row(i, at) for i in range(7)]
             c, e, w, s, d, back, parity = coefs
             here = parity > 0.5
-            s_above, d_above, above = before
+            s_above, d_above, above = before or (None, None, None)
             new, next_level, next_down = [], [], []
             for g in range(groups):
                 span = slice(8 * g, 8 * g + 8)
                 v = now[at, span, :]
                 v_east = pltpu.roll(v, LANES - 1, 1)
                 v_west = pltpu.roll(v, 1, 1)
-                value = level[g] + s_above * v + d_above * jnp.where(above, v_east, v_west)
-                new.append(value * 0.5 if position == 1 else value)
-                value = c * v + e * v_east + w * v_west + down[g]
-                next_level.append(value if position == 1 else value - older[at, span, :])
-                next_down.append(s * v + back * jnp.where(here, v_west, v_east))
+                if has_new:
+                    value = level[g] + s_above * v + d_above * jnp.where(above, v_east, v_west)
+                    new.append(value * 0.5 if position == 1 else value)
+                if has_level:
+                    value = c * v + e * v_east + w * v_west + down[g]
+                    next_level.append(value if position == 1 else value - older[at, span, :])
+                if has_down:
+                    next_down.append(s * v + back * jnp.where(here, v_west, v_east))
+            if not has_new:
+                return tuple(next_level), tuple(next_down), (s, d, here)
             if not last:
                 for g in range(groups):
                     newer[at - 1, 8 * g:8 * g + 8, :] = new[g]
@@ -260,6 +265,18 @@
             return tuple(next_level), tuple(next_down), (s, d, here)
 
         counts = [-(-(count + 2 - 2 * position) // trips) for _, count in regions]
+
+        def at_once():
+            for j in range(max(counts)):
+                for n, count in enumerate(counts):
+                    if j < count:
+                        at = regions[n][0] + position + j
+                        left[n] = one_row(at, *left[n], j > 1, 0 < j < count - 1, j < count - 1)
+
+        left = [((), (), None)] * len(regions)
+        if trips == 1:
+            at_once()
+            return
 
         def several(trip, carry):
             states = []
@@ -522,6 +539,7 @@
     vmem = pl.BlockSpec(memory_space=pltpu.VMEM)
     smem = pl.BlockSpec(memory_space=pltpu.SMEM)
     hbm = pl.BlockSpec(memory_space=pltpu.HBM)
+    anywhere = pl.BlockSpec(memory_space=pl.ANY)
     shape = jax.ShapeDtypeStruct
 
     def packed(count):
@@ -541,7 +559,7 @@
         head_kernel,
         out_shape=(packed(per_row), packed(per_row), shape((6, per_row, PACKED, LANES), BF16), half_rows, half_rows),
         in_specs=[smem] + [hbm] * 5,
-        out_specs=(hbm,) * 5,
+        out_specs=(anywhere,) * 5,
         scratch_shapes=[
             pltpu.VMEM(signal.shape, BF16),
             pltpu.VMEM(signal.shape, BF16),

time: 47.4 us -> 47.4 us (level)
  no operation moved by 1% of the time
where the time goes in v3:
time: 47.4 us; the launch traced here: 47.2 us
  Pallas kernels  27.8 us (59%)
  starting transfers between devices  16 us (34%)
  local copies, waits for them, and re-layouts  1.3 us (3%)
  waiting for transfers between devices  1.21 us (3%)
  between operations  0.89 us (2%)
    pallas_call x2, Pallas kernels, run_main_forward(): pl.pallas_call(functools.partial(main_forward, is_upper, order), out_shap...  7.09 us
    pallas_call x2, Pallas kernels, run_backward_half(): pl.pallas_call(functools.partial(main_backward, is_upper, order), out_sha...  6.57 us
    ppermute x5, starting transfers between devices, on_device(): lax.ppermute(share, *rounds[number])  5.91 us
    ppermute x1, starting transfers between devices, on_device(): lat_second = lax.ppermute(lat_second, 'lat', other_pairs)  4.58 us
    pallas_call x1, Pallas kernels, on_device(): pl.pallas_call(head_kernel, out_shape=(packed(per_row), packed(per_row),...  4.47 us
    pallas_call x1, Pallas kernels, on_device(): pl.pallas_call(functools.partial(edge_forward, order), out_shape=(shape((...  3.52 us
    ppermute x1, starting transfers between devices, on_device(): lon_second = lax.ppermute(lon_second, 'lon', other_pairs)  3.29 us
    pallas_call x2, Pallas kernels, assemble(): pl.pallas_call(assemble_kernel, out_shape=(shape(signal.shape, BF16), gra...  2.87 us
  transfers between devices with their start and end apart: 9, of which 1 were waited for; matrix products, arithmetic and copies ran while one was open for 0% of the time, Pallas kernels for 39%

profile of v3, /device:TPU:1, one launch (start us, length us, event | category | flops | bytes accessed | tf_op | source)
XLA Modules:
  0.0 47.2 jit_solution(7402293896727979476)
XLA Ops:
  0.7 4.5 %head.1 = (bf16[4,80,128]{2,1,0:T(8,128)(2,1)}, bf16[4,80,128]{2,1,0:T(8,128)(2,1)}, bf16[6,4,80,128]{3,2,1,0:T(8,128)(2,1)}, bf16[15,4,80,128]{3,2,1,0:T(8,128)(2,1)}, bf16[15,4,80,128]{3,2,1,0:T(8,128)(2,1)}) custom-call(s32[1]{0:T(128)} %bitcast.place, bf16[32,96,128]{2,1,0:T(8,128)(2,1)} %signal_hbm.1, bf16[32,96,128]{2,1,0:T(8,128)(2,1)} %cotangent_hbm.1, ...), custom_call_target="tpu_custom_call" | custom-call | tf_op jit(solution)/shard_map/head/pallas_call | solution.py:558
  5.1 2.1 %collective-permute-start = (bf16[4,80,128]{2,1,0:T(8,128)(2,1)}, bf16[4,80,128]{2,1,0:T(8,128)(2,1)S(1)}, u32[]{:S(2)}, u32[]{:S(2)}) collective-permute-start(bf16[4,80,128]{2,1,0:T(8,128)(2,1)} %get-tuple-element.31), channel_id=1, source_target_pairs={{0,1},{1,0},{2,3},{3,2},{4,5},{5,4},{6,7},{7,6},{8,9},{9,8},{10,11... | collective-permute-start | bytes 245768 | tf_op jit(solution)/shard_map/ppermute | solution.py:585
  7.2 3.3 %collective-permute-start.1 = (bf16[4,80,128]{2,1,0:T(8,128)(2,1)}, bf16[4,80,128]{2,1,0:T(8,128)(2,1)S(1)}, u32[]{:S(2)}, u32[]{:S(2)}) collective-permute-start(bf16[4,80,128]{2,1,0:T(8,128)(2,1)} %get-tuple-element.32), channel_id=1, source_target_pairs={{0,7},{1,2},{2,1},{3,4},{4,3},{5,6},{6,5},{7,0},{8,15},{9,10},{10,... | collective-permute-start | bytes 245768 | tf_op jit(solution)/shard_map/ppermute | solution.py:586
  10.5 1.3 %copy-done = bf16[15,4,80,128]{3,2,1,0:T(8,128)(2,1)S(1)} copy-done((bf16[15,4,80,128]{3,2,1,0:T(8,128)(2,1)S(1)}, bf16[15,4,80,128]{3,2,1,0:T(8,128)(2,1)}, u32[]{:S(2)}) %copy-start) | copy-done | bytes 1228824
  11.8 3.5 %forward_upper.1 = (bf16[48,32,128]{2,1,0:T(8,128)(2,1)S(1)}, f32[32,192]{1,0:T(8,128)S(1)}) custom-call(bf16[60,80,128]{2,1,0:T(8,128)(2,1)S(1)} %bitcast.4, bf16[60,80,128]{2,1,0:T(8,128)(2,1)S(1)} %bitcast.5), custom_call_target="tpu_custom_call" | custom-call | bytes 12582912 | tf_op jit(solution)/shard_map/forward_upper/pallas_call | solution.py:601
  15.4 0.0 collective-permute-done.lon_first
  15.4 0.6 %merge.1 = (bf16[24,80,128]{2,1,0:T(8,128)(2,1)S(1)}, bf16[7,80,128]{2,1,0:T(8,128)(2,1)S(1)}, bf16[7,80,128]{2,1,0:T(8,128)(2,1)S(1)}) custom-call(s32[1]{0:T(128)} %bitcast.place, bf16[24,80,128]{2,1,0:T(8,128)(2,1)S(1)} %bitcast.14, bf16[60,80,128]{2,1,0:T(8,128)(2,1)S(1)} %bitcast.6, bf16[60,80,128]{2,1,0:T(8,128)(2,1)S(1)} %bitcast.10, ...), custom_call_target="tpu_custom_call" | custom-call | tf_op jit(solution)/shard_map/merge/pallas_call | solution.py:614
  16.1 4.6 %collective-permute-start.3 = (bf16[7,80,128]{2,1,0:T(8,128)(2,1)S(1)}, bf16[7,80,128]{2,1,0:T(8,128)(2,1)S(1)}, u32[]{:S(2)}, u32[]{:S(2)}) collective-permute-start(bf16[7,80,128]{2,1,0:T(8,128)(2,1)S(1)} %get-tuple-element.37), channel_id=1, source_target_pairs={{8,16},{16,8},{9,17},{17,9},{10,18},{18,10},{11,19},{19,11},{12,20... | collective-permute-start | bytes 430088 | tf_op jit(solution)/shard_map/ppermute | solution.py:627
  20.7 0.1 collective-permute-start.2
  20.7 3.6 %forward_lower.1 = (bf16[48,32,128]{2,1,0:T(8,128)(2,1)S(1)}, f32[32,192]{1,0:T(8,128)S(1)}) custom-call(bf16[60,80,128]{2,1,0:T(8,128)(2,1)S(1)} %bitcast.11, bf16[7,80,128]{2,1,0:T(8,128)(2,1)S(1)} %get-tuple-element.34._), custom_call_target="tpu_custom_call" | custom-call | bytes 12582912 | tf_op jit(solution)/shard_map/forward_lower/pallas_call | solution.py:601
  24.3 3.5 %edge_forward.1 = (bf16[34,32,128]{2,1,0:T(8,128)(2,1)S(1)}, f32[32,192]{1,0:T(8,128)S(1)}) custom-call(s32[1]{0:T(128)} %bitcast.place, bf16[24,80,128]{2,1,0:T(8,128)(2,1)S(1)} %get-tuple-element.36.strips_in, bf16[60,80,128]{2,1,0:T(8,128)(2,1)S(1)} %bitcast.7, bf16[60,80,128]{2,1,0:T(8,128)(2,1)S(1)} %bitcast.12, ...), custom_call_target="tpu_custom_call" | custom-call | bytes 12582912 | tf_op jit(solution)/shard_map/edge_forward/pallas_call | solution.py:630
  27.9 0.1 collective-permute-start.4
  28.0 3.2 %backward_upper.1 = (bf16[48,32,128]{2,1,0:T(8,128)(2,1)S(1)}, f32[32,192]{1,0:T(8,128)S(1)}) custom-call(s32[1]{0:T(128)} %bitcast.place, bf16[60,80,128]{2,1,0:T(8,128)(2,1)S(1)} %bitcast.8, bf16[7,80,128]{2,1,0:T(8,128)(2,1)S(1)} %collective-permute-done.2.lat_first, bf16[7,80,128]{2,1,0:T(8,128)(2,1)S(1)} %collective-permute-done.3.lat_second, ...), custom_call_target="tpu_custom_call" | custom-call | bytes 12582912 | tf_op jit(solution)/shard_map/backward_upper/pallas_call | solution.py:653
  31.2 0.5 %collective-permute-start.5 = (f32[32,192]{1,0:T(8,128)S(1)}, f32[32,192]{1,0:T(8,128)S(1)}, u32[]{:S(2)}, u32[]{:S(2)}) collective-permute-start(f32[32,192]{1,0:T(8,128)S(1)} %add.37.summed), channel_id=1, source_target_pairs={{0,2},{1,3},{2,0},{3,1},{4,6},{5,7},{6,4},{7,5},{8,10},{9,11},{10,... | collective-permute-start | bytes 73736 | tf_op jit(solution)/shard_map/ppermute | solution.py:710
  31.7 3.4 %backward_lower.1 = (bf16[48,32,128]{2,1,0:T(8,128)(2,1)S(1)}, f32[32,192]{1,0:T(8,128)S(1)}) custom-call(s32[1]{0:T(128)} %bitcast.place, bf16[60,80,128]{2,1,0:T(8,128)(2,1)S(1)} %bitcast.13, bf16[7,80,128]{2,1,0:T(8,128)(2,1)S(1)} %collective-permute-done.2.lat_first, bf16[7,80,128]{2,1,0:T(8,128)(2,1)S(1)} %collective-permute-done.3.lat_second, ...), custom_call_target="tpu_custom_call" | custom-call | bytes 12582912 | tf_op jit(solution)/shard_map/backward_lower/pallas_call | solution.py:653
  35.1 0.0 collective-permute-done.5
  35.2 2.3 %collective-permute-start.6 = (f32[32,192]{1,0:T(8,128)S(1)}, f32[32,192]{1,0:T(8,128)S(1)}, u32[]{:S(2)}, u32[]{:S(2)}) collective-permute-start(f32[32,192]{1,0:T(8,128)S(1)} %add.38.summed), channel_id=1, source_target_pairs={{0,4},{1,5},{2,6},{3,7},{4,0},{5,1},{6,2},{7,3},{8,12},{9,13},{10,... | collective-permute-start | bytes 73736 | tf_op jit(solution)/shard_map/ppermute | solution.py:710
  37.5 1.9 %edge_backward.1 = (bf16[24,32,128]{2,1,0:T(8,128)(2,1)S(1)}, f32[32,192]{1,0:T(8,128)S(1)}) custom-call(s32[1]{0:T(128)} %bitcast.place, bf16[24,80,128]{2,1,0:T(8,128)(2,1)S(1)} %get-tuple-element.36.strips_in, bf16[60,80,128]{2,1,0:T(8,128)(2,1)S(1)} %bitcast.9, bf16[7,80,128]{2,1,0:T(8,128)(2,1)S(1)} %collective-permute-done.2.lat_first, ...), custom_call_target="tpu_custom_call" | custom-call | bytes 12582912 | tf_op jit(solution)/shard_map/edge_backward/pallas_call | solution.py:666
  39.4 0.2 collective-permute-start.7
  39.6 1.5 %assemble_forward.1 = (bf16[32,96,128]{2,1,0:T(8,128)(2,1)}, f32[32,192]{1,0:T(8,128)S(1)}) custom-call(bf16[48,32,128]{2,1,0:T(8,128)(2,1)S(1)} %get-tuple-element.28.upper, bf16[48,32,128]{2,1,0:T(8,128)(2,1)S(1)} %get-tuple-element.35.lower, bf16[34,32,128]{2,1,0:T(8,128)(2,1)S(1)} %get-tuple-element.38.edges, f32[32,192]{1,0:T(8,128)S(1)} %add.39.summed), custom_call_target="tpu_custom_call" | custom-call | bytes 8388608 | tf_op jit(solution)/shard_map/assemble_forward/pallas_call | solution.py:679
  41.1 1.2 %collective-permute-done.7 = f32[32,192]{1,0:T(8,128)S(1)} collective-permute-done((f32[32,192]{1,0:T(8,128)S(1)}, f32[32,192]{1,0:T(8,128)S(1)}, u32[]{:S(2)}, u32[]{:S(2)}) %collective-permute-start.7) | collective-permute-done | bytes 24608 | tf_op jit(solution)/shard_map/ppermute | solution.py:710
  42.3 2.8 %collective-permute-start.8 = (f32[32,192]{1,0:T(8,128)S(1)}, f32[32,192]{1,0:T(8,128)S(1)}, u32[]{:S(2)}, u32[]{:S(2)}) collective-permute-start(f32[32,192]{1,0:T(8,128)S(1)} %add.40.summed), channel_id=1, source_target_pairs={{0,8},{8,0},{16,24},{24,16},{1,9},{9,1},{17,25},{25,17},{2,10},{10... | collective-permute-start | bytes 73736 | tf_op jit(solution)/shard_map/ppermute | solution.py:710
  45.1 1.4 %assemble_backward.1 = (bf16[32,96,128]{2,1,0:T(8,128)(2,1)}, f32[32,192]{1,0:T(8,128)S(1)}) custom-call(bf16[48,32,128]{2,1,0:T(8,128)(2,1)S(1)} %get-tuple-element.45.upper, bf16[48,32,128]{2,1,0:T(8,128)(2,1)S(1)} %get-tuple-element.46.lower, bf16[24,32,128]{2,1,0:T(8,128)(2,1)S(1)} %get-tuple-element.47.edges, f32[32,192]{1,0:T(8,128)S(1)} %add.40.summed), custom_call_target="tpu_custom_call" | custom-call | bytes 8388608 | tf_op jit(solution)/shard_map/assemble_backward/pallas_call | solution.py:679
  46.5 0.7 %finish.1 = f32[6,32,32]{2,1,0:T(8,128)} custom-call(f32[32,192]{1,0:T(8,128)S(1)} %get-tuple-element.50.mine, f32[32,192]{1,0:T(8,128)S(1)} %collective-permute-done.8.theirs), custom_call_target="tpu_custom_call" | custom-call | tf_op jit(solution)/shard_map/finish/pallas_call | solution.py:715
  (18 shorter events, 0.1 us)
Async XLA Ops:
  5.1 10.2 %collective-permute-start = (bf16[4,80,128]{2,1,0:T(8,128)(2,1)}, bf16[4,80,128]{2,1,0:T(8,128)(2,1)S(1)}, u32[]{:S(2)}, u32[]{:S(2)}) collective-permute-start(bf16[4,80,128]{2,1,0:T(8,128)(2,1)} %get-tuple-element.31), channel_id=1, source_target_pairs={{0,1},{1,0},{2,3},{3,2},{4,5},{5,4},{6,7},{7,6},{8,9},{9,8},{10,11... | collective-permute-start | bytes 245768 | tf_op jit(solution)/shard_map/ppermute | solution.py:585
  7.2 8.1 %collective-permute-start.1 = (bf16[4,80,128]{2,1,0:T(8,128)(2,1)}, bf16[4,80,128]{2,1,0:T(8,128)(2,1)S(1)}, u32[]{:S(2)}, u32[]{:S(2)}) collective-permute-start(bf16[4,80,128]{2,1,0:T(8,128)(2,1)} %get-tuple-element.32), channel_id=1, source_target_pairs={{0,7},{1,2},{2,1},{3,4},{4,3},{5,6},{6,5},{7,0},{8,15},{9,10},{10,... | collective-permute-start | bytes 245768 | tf_op jit(solution)/shard_map/ppermute | solution.py:586
  10.5 1.3 %copy-start = (bf16[15,4,80,128]{3,2,1,0:T(8,128)(2,1)S(1)}, bf16[15,4,80,128]{3,2,1,0:T(8,128)(2,1)}, u32[]{:S(2)}) copy-start(bf16[15,4,80,128]{3,2,1,0:T(8,128)(2,1)} %get-tuple-element.27) | copy-start | bytes 3686404
  11.8 3.6 %copy-start.2 = (bf16[15,4,80,128]{3,2,1,0:T(8,128)(2,1)S(1)}, bf16[15,4,80,128]{3,2,1,0:T(8,128)(2,1)}, u32[]{:S(2)}) copy-start(bf16[15,4,80,128]{3,2,1,0:T(8,128)(2,1)} %get-tuple-element.29) | copy-start | bytes 3686404
  11.8 3.6 %copy-start.3 = (bf16[6,4,80,128]{3,2,1,0:T(8,128)(2,1)S(1)}, bf16[6,4,80,128]{3,2,1,0:T(8,128)(2,1)}, u32[]{:S(2)}) copy-start(bf16[6,4,80,128]{3,2,1,0:T(8,128)(2,1)} %get-tuple-element.30) | copy-start | bytes 1474564
  16.1 8.3 %copy-start.1 = (bf16[15,4,80,128]{3,2,1,0:T(8,128)(2,1)S(1)}, bf16[15,4,80,128]{3,2,1,0:T(8,128)(2,1)}, u32[]{:S(2)}) copy-start(bf16[15,4,80,128]{3,2,1,0:T(8,128)(2,1)} %get-tuple-element.27) | copy-start | bytes 3686404
  16.1 8.2 %collective-permute-start.3 = (bf16[7,80,128]{2,1,0:T(8,128)(2,1)S(1)}, bf16[7,80,128]{2,1,0:T(8,128)(2,1)S(1)}, u32[]{:S(2)}, u32[]{:S(2)}) collective-permute-start(bf16[7,80,128]{2,1,0:T(8,128)(2,1)S(1)} %get-tuple-element.37), channel_id=1, source_target_pairs={{8,16},{16,8},{9,17},{17,9},{10,18},{18,10},{11,19},{19,11},{12,20... | collective-permute-start | bytes 430088 | tf_op jit(solution)/shard_map/ppermute | solution.py:627
  20.7 3.7 %collective-permute-start.2 = (bf16[7,80,128]{2,1,0:T(8,128)(2,1)S(1)}, bf16[7,80,128]{2,1,0:T(8,128)(2,1)S(1)}, u32[]{:S(2)}, u32[]{:S(2)}) collective-permute-start(bf16[7,80,128]{2,1,0:T(8,128)(2,1)S(1)} %get-tuple-element.34._), channel_id=1, source_target_pairs={{0,8},{8,0},{16,24},{24,16},{1,9},{9,1},{17,25},{25,17},{2,10},{10... | collective-permute-start | bytes 430088 | tf_op jit(solution)/shard_map/ppermute | solution.py:626
  27.9 3.3 %collective-permute-start.4 = (f32[32,192]{1,0:T(8,128)S(1)}, f32[32,192]{1,0:T(8,128)S(1)}, u32[]{:S(2)}, u32[]{:S(2)}) collective-permute-start(f32[32,192]{1,0:T(8,128)S(1)} %add_add_fusion.summed), channel_id=1, source_target_pairs={{0,1},{1,0},{2,3},{3,2},{4,5},{5,4},{6,7},{7,6},{8,9},{9,8},{10,11... | collective-permute-start | bytes 73736 | tf_op jit(solution)/shard_map/ppermute | solution.py:710
  31.2 4.0 %collective-permute-start.5 = (f32[32,192]{1,0:T(8,128)S(1)}, f32[32,192]{1,0:T(8,128)S(1)}, u32[]{:S(2)}, u32[]{:S(2)}) collective-permute-start(f32[32,192]{1,0:T(8,128)S(1)} %add.37.summed), channel_id=1, source_target_pairs={{0,2},{1,3},{2,0},{3,1},{4,6},{5,7},{6,4},{7,5},{8,10},{9,11},{10,... | collective-permute-start | bytes 73736 | tf_op jit(solution)/shard_map/ppermute | solution.py:710
  35.2 4.2 %collective-permute-start.6 = (f32[32,192]{1,0:T(8,128)S(1)}, f32[32,192]{1,0:T(8,128)S(1)}, u32[]{:S(2)}, u32[]{:S(2)}) collective-permute-start(f32[32,192]{1,0:T(8,128)S(1)} %add.38.summed), channel_id=1, source_target_pairs={{0,4},{1,5},{2,6},{3,7},{4,0},{5,1},{6,2},{7,3},{8,12},{9,13},{10,... | collective-permute-start | bytes 73736 | tf_op jit(solution)/shard_map/ppermute | solution.py:710
  39.4 2.8 %collective-permute-start.7 = (f32[32,192]{1,0:T(8,128)S(1)}, f32[32,192]{1,0:T(8,128)S(1)}, u32[]{:S(2)}, u32[]{:S(2)}) collective-permute-start(f32[32,192]{1,0:T(8,128)S(1)} %add.39.summed), channel_id=1, source_target_pairs={{0,16},{8,24},{16,0},{24,8},{1,17},{9,25},{17,1},{25,9},{2,18},{10... | collective-permute-start | bytes 73736 | tf_op jit(solution)/shard_map/ppermute | solution.py:710
  42.3 4.2 %collective-permute-start.8 = (f32[32,192]{1,0:T(8,128)S(1)}, f32[32,192]{1,0:T(8,128)S(1)}, u32[]{:S(2)}, u32[]{:S(2)}) collective-permute-start(f32[32,192]{1,0:T(8,128)S(1)} %add.40.summed), channel_id=1, source_target_pairs={{0,8},{8,0},{16,24},{24,16},{1,9},{9,1},{17,25},{25,17},{2,10},{10... | collective-permute-start | bytes 73736 | tf_op jit(solution)/shard_map/ppermute | solution.py:710
